TPU v7x, 32 devices: a whole 2x2x4 slice. The times are simulated.
32 devices in a mesh: tx: 4 (over z), ty: 8 (over y, x, core).
Axes of the slice: x: 2, y: 2, z: 4, core: 2. Of those that a mesh axis runs over, the one named last changes fastest.
Arguments:
- reduced_heat: float32 [8, 256, 512], P(None, 'ty', 'tx'), may hold values from 0.3 to 1.2
- substance_kind: int32 [8, 256, 512], P(None, 'ty', 'tx'), may hold values from 0 to 3
- moment_vector: float32 [3, 8, 256, 512], P(None, None, 'ty', 'tx'), may hold values from -4 to 4
- stray_tensor: float32 [6, 16, 512, 1024], P(None, 'tx', None, 'ty'), may hold values from -8 to 8
- diffusivity_nodes: float32 [16], replicated, may hold values from 0.5 to 1.5
- substance_factor: float32 [4], replicated, may hold values from 0.5 to 2
- ordering_threshold: float32 [4], replicated, may hold values from 0.7 to 1.1
- beam_transverse_spot: int32 [2], replicated, may hold values from 0 to 255
- beam_downtrack_spot: int32 [2], replicated, may hold values from 0 to 511
Outputs:
- warmed_state: float32 [8, 256, 512], P(None, 'ty', 'tx')
- demag_field: float32 [3, 8, 256, 512], P(None, None, 'ty', 'tx')
All inputs are finite; a program needn't handle non-finite values.
Results may differ from a plain program's by a relative error of at most 0.00007.
Values sent between devices are 32-bit elements; how exact they have to be, the bound alone decides.
A program may use at most 128 MiB of HBM per device.

v0:
```python
import math

import jax
import jax.numpy as jnp
from jax import lax
from jax.sharding import PartitionSpec as P

SWEEPS = 2


AMBIENT_HEAT = 0.3
STEP_RATE = 0.05
LASER_POWER = 4.0
LASER_DEPTH = 4.0
ORDERING_SPREAD = 0.08
TABLE_LOW = 0.2
TABLE_SPAN = 1.6
RADIX_PARTS = 16
HIGHEST = lax.Precision.HIGHEST


def extended(value, sides, width, wrap):
    for axis, dim in sides:
        count, length = (lax.axis_size(axis), value.shape[dim])
        up = [(i, (i + 1) % count) for i in range(count if wrap else count - 1)]
        down = [(j, i) for i, j in up]
        last = lax.slice_in_dim(value, length - width, length, axis=dim)
        first = lax.slice_in_dim(value, 0, width, axis=dim)
        before = lax.ppermute(last, axis, up)
        after = lax.ppermute(first, axis, down)
        value = jnp.concatenate([before, value, after], axis=dim)
    return value


def lookup_diffusivity(absolute, diffusivity_nodes):
    nodes = diffusivity_nodes.shape[0]
    spacing = TABLE_SPAN / (nodes - 1)
    total = jnp.zeros_like(absolute) + diffusivity_nodes[0]
    for index in range(nodes - 1):
        start_node = TABLE_LOW + index * spacing
        total = total + (diffusivity_nodes[index + 1] - diffusivity_nodes[index]) * jnp.clip(
            (absolute - start_node) / spacing, 0.0, 1.0
        )
    return total


def per_particle(substance_kind, values):
    result = jnp.zeros(substance_kind.shape, jnp.float32)
    for grain in range(values.shape[0]):
        result = result + jnp.where(substance_kind == grain, values[grain], 0.0)
    return result


def laser_heating(
    row_ids, col_ids, sheet_indices, spot_row, spot_col, total_cols, col_width, row_width
):
    along = ((col_ids - spot_col + total_cols // 2) % total_cols - total_cols // 2).astype(
        jnp.float32
    ) / col_width
    across = (row_ids - spot_row).astype(jnp.float32) / row_width
    col_factor = jnp.exp(-0.5 * along * along)
    row_factor = jnp.exp(-0.5 * across * across)
    layer_factor = jnp.exp(-jnp.arange(sheet_indices, dtype=jnp.float32) / LASER_DEPTH)
    return layer_factor[:, None, None] * row_factor[None, :, None] * col_factor[None, None, :]


def heat_update(center, diffusivity, neighbours, heating):
    flux = jnp.zeros_like(center)
    for other_temp, other_cond in neighbours:
        flux = flux + 0.5 * (diffusivity + other_cond) * (other_temp - center)
    vertical = 0.5 * (diffusivity[1:] + diffusivity[:-1]) * (center[1:] - center[:-1])
    zero_layer = jnp.zeros_like(center[:1])
    flux = (
        flux
        + jnp.concatenate([vertical, zero_layer], 0)
        - jnp.concatenate([zero_layer, vertical], 0)
    )
    return center + STEP_RATE * (flux + LASER_POWER * heating)


def phase_table(count_in, width, length):
    inputs = jnp.arange(count_in, dtype=jnp.int32)[:, None]
    outputs = jnp.arange(width, dtype=jnp.int32)[None, :]
    angles = (inputs * outputs % length).astype(jnp.float32) * (2.0 * math.pi / length)
    return (jnp.cos(angles), jnp.sin(angles))


def signed_table(rows_count, cols_count, modulus, sign):
    cosine, sine = phase_table(rows_count, cols_count, modulus)
    return (cosine, sign * sine)


def complex_product(form, real_part, imag_part, cosine, sine):

    def product(values, table):
        return jnp.einsum(form, values, table, precision=HIGHEST)

    return (
        product(real_part, cosine) - product(imag_part, sine),
        product(real_part, sine) + product(imag_part, cosine),
    )


def sectioned_dft(real_part, imag_part, count_out, length, sign, on_rows):
    count_in = real_part.shape[-2] if on_rows else real_part.shape[-1]
    span = length // RADIX_PARTS
    first_in = count_in // span
    last_out = count_out // RADIX_PARTS
    first_cos, first_sin = signed_table(first_in, RADIX_PARTS, RADIX_PARTS, sign)
    twist_cos, twist_sin = signed_table(RADIX_PARTS, span, length, sign)
    second_cos, second_sin = signed_table(span, last_out, span, sign)
    if on_rows:
        lead = real_part.shape[:-2]
        tail = real_part.shape[-1]
        split = lead + (first_in, span, tail)
        joined = lead + (last_out * RADIX_PARTS, tail)
        first_form = "...pqx,pk->...kqx"
        second_form = "...kqx,qm->...mkx"
        twist_cos = twist_cos[:, :, None]
        twist_sin = twist_sin[:, :, None]
    else:
        lead = real_part.shape[:-1]
        split = lead + (first_in, span)
        joined = lead + (last_out * RADIX_PARTS,)
        first_form = "...pq,pk->...kq"
        second_form = "...kq,qm->...mk"
    real_part, imag_part = complex_product(
        first_form, real_part.reshape(split), imag_part.reshape(split), first_cos, first_sin
    )
    real_part, imag_part = (
        real_part * twist_cos - imag_part * twist_sin,
        real_part * twist_sin + imag_part * twist_cos,
    )
    real_part, imag_part = complex_product(
        second_form, real_part, imag_part, second_cos, second_sin
    )
    return (real_part.reshape(joined), imag_part.reshape(joined))


def along_last(spectra, count_out, length, sign, factor):
    out_real, out_imag = sectioned_dft(spectra[0], spectra[1], count_out, length, sign, False)
    return jnp.stack([out_real, out_imag]) * factor


def along_rows(spectra, count_out, length, sign, factor):
    out_real, out_imag = sectioned_dft(spectra[0], spectra[1], count_out, length, sign, True)
    return jnp.stack([out_real, out_imag]) * factor


def forward_layers(values, cosine, sine):
    out_real = jnp.einsum("czyx,zk->ckyx", values, cosine, precision=HIGHEST)
    out_imag = -jnp.einsum("czyx,zk->ckyx", values, sine, precision=HIGHEST)
    return jnp.stack([out_real, out_imag])


def apply_kernel(stray_tensor, spectra):
    pairs = ((0, 3, 4), (3, 1, 5), (4, 5, 2))
    fields = []
    for target in range(3):
        total = (
            stray_tensor[pairs[target][0]] * spectra[:, 0]
            + stray_tensor[pairs[target][1]] * spectra[:, 1]
            + stray_tensor[pairs[target][2]] * spectra[:, 2]
        )
        fields.append(-total)
    return jnp.stack(fields, axis=1)


def local(
    reduced_heat,
    substance_kind,
    moment_vector,
    stray_tensor,
    diffusivity_nodes,
    substance_factor,
    ordering_threshold,
    beam_transverse_spot,
    beam_downtrack_spot,
):
    sheet_indices, downtrack_indices, transverse_indices = reduced_heat.shape
    total_rows = downtrack_indices * lax.axis_size("ty")
    total_cols = transverse_indices * lax.axis_size("tx")
    row_base = lax.axis_index("ty") * downtrack_indices
    col_base = lax.axis_index("tx") * transverse_indices
    rotation_phase = reduced_heat - AMBIENT_HEAT
    site_multiplier = per_particle(substance_kind, substance_factor)
    row_ids = row_base + jnp.arange(downtrack_indices, dtype=jnp.int32)
    col_ids = col_base + jnp.arange(transverse_indices, dtype=jnp.int32)
    for sweep in range(SWEEPS):
        diffusivity = site_multiplier * lookup_diffusivity(
            rotation_phase + AMBIENT_HEAT, diffusivity_nodes
        )
        fields = jnp.stack([rotation_phase, diffusivity])
        along = extended(fields, (("tx", 3),), 1, True)
        across = extended(fields, (("ty", 2),), 1, False)
        neighbours = [
            (along[0, :, :, :-2], along[1, :, :, :-2]),
            (along[0, :, :, 2:], along[1, :, :, 2:]),
            (across[0, :, :-2], across[1, :, :-2]),
            (across[0, :, 2:], across[1, :, 2:]),
        ]
        heating = laser_heating(
            row_ids,
            col_ids,
            sheet_indices,
            beam_transverse_spot[sweep],
            beam_downtrack_spot[sweep],
            total_cols,
            0.5 * transverse_indices,
            1.0 * downtrack_indices,
        )
        rotation_phase = heat_update(rotation_phase, diffusivity, neighbours, heating)
    warmed_state = rotation_phase + AMBIENT_HEAT
    proportion = jax.nn.sigmoid(
        (per_particle(substance_kind, ordering_threshold) - warmed_state) / ORDERING_SPREAD
    )
    scaled = moment_vector * proportion[None]
    double_layers = 2 * sheet_indices
    layer_cos, layer_sin = phase_table(sheet_indices, double_layers, double_layers)
    spectra = forward_layers(scaled, layer_cos, layer_sin)
    spectra = lax.all_to_all(spectra, "tx", split_axis=2, concat_axis=4, tiled=True)
    spectra = along_last(spectra, 2 * total_cols, 2 * total_cols, -1, 1.0)
    spectra = lax.all_to_all(spectra, "ty", split_axis=4, concat_axis=3, tiled=True)
    spectra = along_rows(spectra, 2 * total_rows, 2 * total_rows, -1, 1.0)
    field = apply_kernel(stray_tensor, spectra)
    field = along_rows(field, total_rows, 2 * total_rows, 1, 1.0 / (2 * total_rows))
    field = lax.all_to_all(field, "ty", split_axis=3, concat_axis=4, tiled=True)
    field = along_last(field, total_cols, 2 * total_cols, 1, 1.0 / (2 * total_cols))
    field = lax.all_to_all(field, "tx", split_axis=4, concat_axis=2, tiled=True)
    back_cos, back_sin = phase_table(double_layers, sheet_indices, double_layers)
    demag_field = (
        jnp.einsum("ckyx,kz->czyx", field[0], back_cos, precision=HIGHEST)
        - jnp.einsum("ckyx,kz->czyx", field[1], back_sin, precision=HIGHEST)
    ) * (1.0 / double_layers)
    return (warmed_state, demag_field)


def solution(mesh):
    in_specs = (
        P(None, "ty", "tx"),
        P(None, "ty", "tx"),
        P(None, None, "ty", "tx"),
        P(None, "tx", None, "ty"),
        P(),
        P(),
        P(),
        P(),
        P(),
    )
    out_specs = (P(None, "ty", "tx"), P(None, None, "ty", "tx"))
    return jax.shard_map(local, mesh=mesh, in_specs=in_specs, out_specs=out_specs, check_vma=False)
```

profile of v0, /device:TPU:2, one launch (start us, length us, event | category | flops | bytes accessed | tf_op | source)
XLA Modules:
  0.0 566.6 jit_solution(5469210464926585680)
XLA Ops:
  74.7 37.1 %all-to-all-done = f32[2,3,16,32,128]{4,3,1,0,2:T(8,128)S(1)} async-done(((f32[2,3,16,32,128]{4,3,1,0,2:T(8,128)}), f32[2,3,16,32,128]{4,3,1,0,2:T(8,128)S(1)}, u32[]{:S(2)}, u32[]{:S(2)}) %all-to-all-start) | async-done | bytes 1572896 | tf_op jit(solution)/shard_map/all_to_all | solution.py:221
  122.9 5.4 convolution_add_fusion.2
  147.2 6.3 %copy.171 = f32[3,4,32,64,16]{2,4,3,1,0:T(8,128)} copy(f32[3,4,32,64,16]{3,2,4,1,0:T(8,128)} %subtract_bitcast_fusion.5) | data formatting | bytes 3145728 | tf_op jit(solution)/shard_map/sub | solution.py:99
  153.5 5.8 %add_bitcast_fusion.5 = f32[3,4,32,64,16]{3,2,4,1,0:T(8,128)} fusion(f32[64,3,4,32,16]{0,3,4,2,1:T(8,128)} %fusion.32, f32[3,4,32,16,64]{4,3,2,1,0:T(8,128)S(1)} %get-tuple-element.31), kind=kOutput, calls=%fused_computation.17 | convolution fusion | flops 302444544 | bytes 4718592 | tf_op jit(solution)/shard_map/...kq,qm->...mk/dot_general | solution.py:96
  159.3 6.1 %copy.174 = f32[3,4,32,64,16]{2,4,3,1,0:T(8,128)} copy(f32[3,4,32,64,16]{3,2,4,1,0:T(8,128)} %add_bitcast_fusion.5) | data formatting | bytes 3145728 | tf_op jit(solution)/shard_map/add | solution.py:100
  165.4 10.5 %pad_maximum_fusion = f32[2,3,4,32,1024]{3,4,2,1,0:T(8,128)} fusion(f32[1,3,4,32,1024]{3,4,2,1,0:T(8,128)} %bitcast.457, f32[1,3,4,32,1024]{3,4,2,1,0:T(8,128)} %bitcast.456), kind=kLoop, calls=%fused_computation | loop fusion | flops 786432 | bytes 6291456 | tf_op jit(solution)/shard_map/stack | solution.py:142
  175.9 16.4 %copy.297 = f32[2,3,4,32,1024]{3,2,1,0,4:T(4,128)} copy(f32[2,3,4,32,1024]{3,4,2,1,0:T(8,128)} %pad_maximum_fusion) | data formatting | bytes 6291456 | tf_op jit(solution)/shard_map/stack | solution.py:142
  192.3 12.3 %reshape.262 = f32[8,1,98304]{2,1,0:T(1,128)} reshape(f32[1024,2,3,4,32]{4,3,2,1,0:T(4,128)} %bitcast.442) | data formatting | bytes 6291456
  208.9 5.5 slice_bitcast_fusion.8
  214.3 29.9 %all-to-all-done.1 = f32[8,1,98304]{2,1,0:T(1,128)S(1)} async-done(((f32[8,1,98304]{2,1,0:T(1,128)}), f32[8,1,98304]{2,1,0:T(1,128)S(1)}, u32[]{:S(2)}, u32[]{:S(2)}) %all-to-all-start.1) | async-done | bytes 3145760 | tf_op jit(solution)/shard_map/all_to_all | solution.py:223
  244.8 11.1 %reduce = f32[8,98304]{1,0:T(8,128)} reduce(f32[8,1,98304]{2,1,0:T(1,128)S(1)} %all-to-all-done.1, f32[]{:T(128)} %broadcast.988), dimensions={1}, to_apply=%all_to_all.47.reduce_sub_computation | reduce | bytes 6291460 | tf_op jit(solution)/shard_map/all_to_all | solution.py:223
  255.9 13.2 %reshape.263 = f32[1024,2,3,4,32]{4,3,2,1,0:T(4,128)} reshape(f32[8,98304]{1,0:T(8,128)} %reduce) | data formatting | bytes 6291456
  269.1 7.6 %copy.226 = f32[2,3,4,32,8,128]{5,4,3,2,1,0:T(8,128)S(1)} copy(f32[2,3,4,32,8,128]{3,2,1,0,5,4:T(4,128)} %bitcast.443) | data formatting | bytes 6291456 | tf_op jit(solution)/shard_map/all_to_all | solution.py:223
  326.7 5.4 subtract_bitcast_fusion.2
  347.1 5.3 all-to-all-start.2
  352.4 36.3 %all-to-all-done.2 = f32[2,3,4,256,128]{4,2,1,0,3:T(4,128)S(1)} async-done(((f32[2,3,4,256,128]{4,2,1,0,3:T(4,128)}), f32[2,3,4,256,128]{4,2,1,0,3:T(4,128)S(1)}, u32[]{:S(2)}, u32[]{:S(2)}) %all-to-all-start.2) | async-done | bytes 3145760 | tf_op jit(solution)/shard_map/all_to_all | solution.py:227
  416.2 5.3 subtract_bitcast_fusion.1
  421.5 14.6 %fusion.2 = f32[32,3,4,32,16]{3,0,4,2,1:T(8,128)S(1)} fusion(f32[3,4,32,16,64]{4,3,2,1,0:T(8,128)S(1)} %get-tuple-element.30), kind=kOutput, calls=%fused_computation.23 | convolution fusion | flops 151023616 | bytes 2359296 | tf_op jit(solution)/shard_map/...kq,qm->...mk/dot_general | solution.py:96
  436.1 16.0 %fusion = f32[32,3,4,32,16]{3,0,4,2,1:T(8,128)} fusion(f32[3,4,32,16,64]{4,3,2,1,0:T(8,128)S(1)} %get-tuple-element.30), kind=kOutput, calls=%fused_computation.21 | convolution fusion | flops 151023616 | bytes 2359296 | tf_op jit(solution)/shard_map/...kq,qm->...mk/dot_general | solution.py:96
  452.1 14.9 %subtract_bitcast_fusion = f32[3,4,32,32,16]{2,3,4,1,0:T(8,128)S(1)} fusion(f32[32,3,4,32,16]{3,0,4,2,1:T(8,128)S(1)} %fusion.2, f32[3,4,32,16,64]{4,3,2,1,0:T(8,128)S(1)} %get-tuple-element.29), kind=kOutput, calls=%fused_computation.8 | convolution fusion | flops 151220224 | bytes 3145728 | tf_op jit(solution)/shard_map/...kq,qm->...mk/dot_general | solution.py:96
  473.9 16.4 %add_bitcast_fusion = f32[3,4,32,32,16]{2,3,4,1,0:T(8,128)S(1)} fusion(f32[32,3,4,32,16]{3,0,4,2,1:T(8,128)} %fusion, f32[3,4,32,16,64]{4,3,2,1,0:T(8,128)S(1)} %get-tuple-element.29), kind=kOutput, calls=%fused_computation.7 | convolution fusion | flops 151220224 | bytes 3145728 | tf_op jit(solution)/shard_map/...kq,qm->...mk/dot_general | solution.py:96
  500.7 6.0 %reshape.264 = f32[4,1,98304]{2,1,0:T(1,128)S(1)} reshape(f32[512,2,3,4,32]{4,3,2,1,0:T(4,128)} %bitcast.458) | data formatting | bytes 3145728
  506.7 40.1 %all_to_all.60 = f32[4,1,98304]{2,1,0:T(1,128)S(1)} all-to-all(f32[4,1,98304]{2,1,0:T(1,128)S(1)} %reshape.264), channel_id=1, replica_groups=mesh['tx'=4,'ty'=8] {'tx'}, dimensions={0} | all-to-all | bytes 3145728 | tf_op jit(solution)/shard_map/all_to_all | solution.py:229
  552.0 6.2 %reshape.265 = f32[512,2,3,4,32]{4,3,2,1,0:T(4,128)} reshape(f32[4,98304]{1,0:T(4,128)S(1)} %reduce.1) | data formatting | bytes 3145728
  (130 shorter events, 212.7 us)
Async XLA Ops:
  28.0 38.7 %copy-start.11 = (f32[3,8,32,128]{3,2,1,0:T(8,128)S(1)}, f32[3,8,32,128]{3,2,1,0:T(8,128)}, u32[]{:S(2)}) copy-start(f32[3,8,32,128]{3,2,1,0:T(8,128)} %param.11) | copy-start | bytes 1179652
  28.2 16.4 %collective-permute-start = (f32[2,8,32,1]{3,2,1,0:T(8,128)S(1)}, f32[2,8,32,1]{3,2,1,0:T(8,128)S(1)}, u32[]{:S(2)}, u32[]{:S(2)}) collective-permute-start(f32[2,8,32,1]{3,2,1,0:T(8,128)S(1)} %get-tuple-element.51), channel_id=1, source_target_pairs={{0,8},{8,16},{16,24},{24,0},{1,9},{9,17},{17,25},{25,1},{2,10},{10... | collective-permute-start | bytes 6152 | tf_op jit(solution)/shard_map/ppermute | solution.py:29
  29.8 14.7 %collective-permute-start.1 = (f32[2,8,32,1]{3,2,1,0:T(8,128)S(1)}, f32[2,8,32,1]{3,2,1,0:T(8,128)S(1)}, u32[]{:S(2)}, u32[]{:S(2)}) collective-permute-start(f32[2,8,32,1]{3,2,1,0:T(8,128)S(1)} %get-tuple-element.52), channel_id=1, source_target_pairs={{8,0},{16,8},{24,16},{0,24},{9,1},{17,9},{25,17},{1,25},{10,2},{18... | collective-permute-start | bytes 6152 | tf_op jit(solution)/shard_map/ppermute | solution.py:30
  32.1 12.5 %collective-permute-start.2 = (f32[2,8,1,128]{3,2,1,0:T(1,128)S(1)}, f32[2,8,1,128]{3,2,1,0:T(1,128)S(1)}, u32[]{:S(2)}, u32[]{:S(2)}) collective-permute-start(f32[2,8,1,128]{3,2,1,0:T(1,128)S(1)} %get-tuple-element.53), channel_id=1, source_target_pairs={{0,1},{1,2},{2,3},{3,4},{4,5},{5,6},{6,7},{8,9},{9,10},{10,11},{11... | collective-permute-start | bytes 24584 | tf_op jit(solution)/shard_map/ppermute | solution.py:29
  34.0 10.6 %collective-permute-start.3 = (f32[2,8,1,128]{3,2,1,0:T(1,128)S(1)}, f32[2,8,1,128]{3,2,1,0:T(1,128)S(1)}, u32[]{:S(2)}, u32[]{:S(2)}) collective-permute-start(f32[2,8,1,128]{3,2,1,0:T(1,128)S(1)} %get-tuple-element.54), channel_id=1, source_target_pairs={{1,0},{2,1},{3,2},{4,3},{5,4},{6,5},{7,6},{9,8},{10,9},{11,10},{12... | collective-permute-start | bytes 24584 | tf_op jit(solution)/shard_map/ppermute | solution.py:30
  49.5 11.0 %collective-permute-start.4 = (f32[2,8,32,1]{3,2,1,0:T(8,128)S(1)}, f32[2,8,32,1]{3,2,1,0:T(8,128)S(1)}, u32[]{:S(2)}, u32[]{:S(2)}) collective-permute-start(f32[2,8,32,1]{3,2,1,0:T(8,128)S(1)} %get-tuple-element.47), channel_id=1, source_target_pairs={{0,8},{8,16},{16,24},{24,0},{1,9},{9,17},{17,25},{25,1},{2,10},{10... | collective-permute-start | bytes 6152 | tf_op jit(solution)/shard_map/ppermute | solution.py:29
  49.5 13.8 %collective-permute-start.5 = (f32[2,8,32,1]{3,2,1,0:T(8,128)S(1)}, f32[2,8,32,1]{3,2,1,0:T(8,128)S(1)}, u32[]{:S(2)}, u32[]{:S(2)}) collective-permute-start(f32[2,8,32,1]{3,2,1,0:T(8,128)S(1)} %get-tuple-element.48), channel_id=1, source_target_pairs={{8,0},{16,8},{24,16},{0,24},{9,1},{17,9},{25,17},{1,25},{10,2},{18... | collective-permute-start | bytes 6152 | tf_op jit(solution)/shard_map/ppermute | solution.py:30
  53.3 9.9 %collective-permute-start.6 = (f32[2,8,1,128]{3,2,1,0:T(1,128)S(1)}, f32[2,8,1,128]{3,2,1,0:T(1,128)S(1)}, u32[]{:S(2)}, u32[]{:S(2)}) collective-permute-start(f32[2,8,1,128]{3,2,1,0:T(1,128)S(1)} %get-tuple-element.49), channel_id=1, source_target_pairs={{0,1},{1,2},{2,3},{3,4},{4,5},{5,6},{6,7},{8,9},{9,10},{10,11},{11... | collective-permute-start | bytes 24584 | tf_op jit(solution)/shard_map/ppermute | solution.py:29
  55.3 8.0 %collective-permute-start.7 = (f32[2,8,1,128]{3,2,1,0:T(1,128)S(1)}, f32[2,8,1,128]{3,2,1,0:T(1,128)S(1)}, u32[]{:S(2)}, u32[]{:S(2)}) collective-permute-start(f32[2,8,1,128]{3,2,1,0:T(1,128)S(1)} %get-tuple-element.50), channel_id=1, source_target_pairs={{1,0},{2,1},{3,2},{4,3},{5,4},{6,5},{7,6},{9,8},{10,9},{11,10},{12... | collective-permute-start | bytes 24584 | tf_op jit(solution)/shard_map/ppermute | solution.py:30
  70.6 41.3 %all-to-all-start = ((f32[2,3,16,32,128]{4,3,1,0,2:T(8,128)}), f32[2,3,16,32,128]{4,3,1,0,2:T(8,128)S(1)}, u32[]{:S(2)}, u32[]{:S(2)}) async-start(f32[2,3,16,32,128]{4,3,1,0,2:T(8,128)} %copy.167), calls=%async_computation | async-start | bytes 3145728 | tf_op jit(solution)/shard_map/all_to_all | solution.py:221
  122.9 5.5 copy-start.1
  122.9 5.5 copy-start.3
  204.6 39.7 %all-to-all-start.1 = ((f32[8,1,98304]{2,1,0:T(1,128)}), f32[8,1,98304]{2,1,0:T(1,128)S(1)}, u32[]{:S(2)}, u32[]{:S(2)}) async-start(f32[8,1,98304]{2,1,0:T(1,128)} %reshape.262), calls=%async_computation.1 | async-start | bytes 6291456 | tf_op jit(solution)/shard_map/all_to_all | solution.py:223
  306.9 2.2 copy-start.4
  306.9 2.2 copy-start.5
  306.9 2.2 copy-start.10
  309.1 1.2 copy-start.7
  309.2 1.5 copy-start.8
  309.2 1.8 copy-start.9
  347.1 41.6 %all-to-all-start.2 = ((f32[2,3,4,256,128]{4,2,1,0,3:T(4,128)}), f32[2,3,4,256,128]{4,2,1,0,3:T(4,128)S(1)}, u32[]{:S(2)}, u32[]{:S(2)}) async-start(f32[2,3,4,256,128]{4,2,1,0,3:T(4,128)} %copy.193), calls=%async_computation.2 | async-start | bytes 6291456 | tf_op jit(solution)/shard_map/all_to_all | solution.py:227
  400.0 4.5 copy-start.6
  409.6 1.7 copy-start
  411.3 4.9 copy-start.2
where the time goes:
time: 573 us; the launch traced here: 567 us
  matrix products  180 us (31%)
  local copies, waits for them, and re-layouts  139 us (24%)
  waiting for transfers between devices  108 us (19%)
  other arithmetic  47.8 us (8%)
  blocking collectives  40.1 us (7%)
  starting transfers between devices  32.3 us (6%)
  between operations  20.1 us (4%)
    dot_general x32, matrix products, product(): return jnp.einsum(form, values, table, precision=HIGHEST)  177 us
    unnamed x29, local copies, waits for them, and re-layouts  41.5 us
    all_to_all x1, blocking collectives, local(): field = lax.all_to_all(field, 'tx', split_axis=4, concat_axis=2, tiled=True)  40.1 us
    all_to_all x1, waiting for transfers between devices, local(): lax.all_to_all(spectra, 'tx', split_axis=2, concat_axis=4, tiled=True)  37.1 us
    all_to_all x1, waiting for transfers between devices, local(): field = lax.all_to_all(field, 'ty', split_axis=3, concat_axis=4, tiled=True)  36.3 us
    all_to_all x1, waiting for transfers between devices, local(): lax.all_to_all(spectra, 'ty', split_axis=4, concat_axis=3, tiled=True)  29.9 us
    another operation x3, local copies, waits for them, and re-layouts, along_last(): return jnp.stack([out_real, out_imag]) * factor  21.4 us
    ppermute x4, starting transfers between devices, extended(): after = lax.ppermute(first, axis, down)  13.3 us
  transfers between devices with their start and end apart: 11, of which 5 were waited for; matrix products, arithmetic and copies ran while one was open for 2% of the time, Pallas kernels for 0%

commit v1 on v0

v1 whole, which is shorter than its diff:
```python
import functools
import math

import jax
import jax.numpy as jnp
import ml_dtypes
import numpy as np
from jax import lax
from jax.experimental import pallas as pl
from jax.experimental.pallas import tpu as pltpu
from jax.sharding import PartitionSpec as P

SWEEPS = 2


AMBIENT_HEAT = 0.3
STEP_RATE = 0.05
LASER_POWER = 4.0
LASER_DEPTH = 4.0
ORDERING_SPREAD = 0.08
TABLE_LOW = 0.2
TABLE_SPAN = 1.6


def extended(value, sides, width, wrap):
    for axis, dim in sides:
        count, length = (lax.axis_size(axis), value.shape[dim])
        up = [(i, (i + 1) % count) for i in range(count if wrap else count - 1)]
        down = [(j, i) for i, j in up]
        last = lax.slice_in_dim(value, length - width, length, axis=dim)
        first = lax.slice_in_dim(value, 0, width, axis=dim)
        before = lax.ppermute(last, axis, up)
        after = lax.ppermute(first, axis, down)
        value = jnp.concatenate([before, value, after], axis=dim)
    return value


def lookup_diffusivity(absolute, diffusivity_nodes):
    nodes = diffusivity_nodes.shape[0]
    spacing = TABLE_SPAN / (nodes - 1)
    total = jnp.zeros_like(absolute) + diffusivity_nodes[0]
    for index in range(nodes - 1):
        start_node = TABLE_LOW + index * spacing
        total = total + (diffusivity_nodes[index + 1] - diffusivity_nodes[index]) * jnp.clip(
            (absolute - start_node) / spacing, 0.0, 1.0
        )
    return total


def per_particle(substance_kind, values):
    result = jnp.zeros(substance_kind.shape, jnp.float32)
    for grain in range(values.shape[0]):
        result = result + jnp.where(substance_kind == grain, values[grain], 0.0)
    return result


def laser_heating(
    row_ids, col_ids, sheet_indices, spot_row, spot_col, total_cols, col_width, row_width
):
    along = ((col_ids - spot_col + total_cols // 2) % total_cols - total_cols // 2).astype(
        jnp.float32
    ) / col_width
    across = (row_ids - spot_row).astype(jnp.float32) / row_width
    col_factor = jnp.exp(-0.5 * along * along)
    row_factor = jnp.exp(-0.5 * across * across)
    layer_factor = jnp.exp(-jnp.arange(sheet_indices, dtype=jnp.float32) / LASER_DEPTH)
    return layer_factor[:, None, None] * row_factor[None, :, None] * col_factor[None, None, :]


def heat_update(center, diffusivity, neighbours, heating):
    flux = jnp.zeros_like(center)
    for other_temp, other_cond in neighbours:
        flux = flux + 0.5 * (diffusivity + other_cond) * (other_temp - center)
    vertical = 0.5 * (diffusivity[1:] + diffusivity[:-1]) * (center[1:] - center[:-1])
    zero_layer = jnp.zeros_like(center[:1])
    flux = (
        flux
        + jnp.concatenate([vertical, zero_layer], 0)
        - jnp.concatenate([zero_layer, vertical], 0)
    )
    return center + STEP_RATE * (flux + LASER_POWER * heating)


MESH = pl.DeviceIdType.MESH
PAIRS = ((0, 3, 4), (3, 1, 5), (4, 5, 2))


def halves(table):
    high = table.astype(ml_dtypes.bfloat16)
    low = (table - high.astype(np.float64)).astype(ml_dtypes.bfloat16)
    return (high, low)


def angles(rows, cols, length):
    grid = np.outer(np.arange(rows), np.arange(cols)) % length
    return grid * (2.0 * math.pi / length)


def blocked_pair(angle, width):
    rows, cols = angle.shape
    cosine = np.cos(angle).reshape(rows, cols // width, width)
    sine = np.sin(angle).reshape(rows, cols // width, width)
    return np.concatenate([cosine, sine], axis=2).transpose(1, 0, 2)


def split(value):
    high = value.astype(jnp.bfloat16)
    return (high, (value - high.astype(jnp.float32)).astype(jnp.bfloat16))


def product(left_high, left_low, right_high, right_low):
    def dot(a, b):
        return jnp.dot(a, b, preferred_element_type=jnp.float32)

    return dot(left_high, right_high) + (dot(left_high, right_low) + dot(left_low, right_high))


def greet(tx, ty, ntx, nty):
    barrier = pltpu.get_barrier_semaphore()
    for step in range(1, ntx):
        pl.semaphore_signal(
            barrier, inc=1, device_id=(lax.rem(tx + step, ntx), ty), device_id_type=MESH
        )
    for step in range(1, nty):
        pl.semaphore_signal(
            barrier, inc=1, device_id=(tx, lax.rem(ty + step, nty)), device_id_type=MESH
        )
    pl.semaphore_wait(barrier, ntx + nty - 2)


def send_over(axis, step, part, source, target, sems, ntx, nty):
    tx, ty = lax.axis_index("tx"), lax.axis_index("ty")
    if axis == "tx":
        dest = lax.rem(tx + step, ntx)
        mine, device = tx, (dest, ty)
    else:
        dest = lax.rem(ty + step, nty)
        mine, device = ty, (tx, dest)
    return pltpu.make_async_remote_copy(
        src_ref=source.at[dest, part],
        dst_ref=target.at[mine, part],
        send_sem=sems[0].at[part, step],
        recv_sem=sems[1].at[part, step],
        device_id=device,
        device_id_type=MESH,
    )


def forward_kernel(
    ntx, nty, scaled, table_high, table_low, out, layered, gathered, left_high, left_low, blocks,
    tx_send, tx_recv, ty_send, ty_recv,
):
    tx, ty = lax.axis_index("tx"), lax.axis_index("ty")
    parts, sheets, rows, width = scaled.shape
    count = 2 * sheets
    own = count // ntx
    tx_sems, ty_sems = (tx_send, tx_recv), (ty_send, ty_recv)

    def over_tx(step, part):
        return send_over("tx", step, part, layered, gathered, tx_sems, ntx, nty)

    def over_ty(step, part):
        return send_over("ty", step, part, blocks, out, ty_sems, ntx, nty)

    def layer_part(part, carry):
        for freq in range(sheets + 1):
            real = jnp.zeros((rows, width), jnp.float32)
            imag = jnp.zeros((rows, width), jnp.float32)
            for sheet in range(sheets):
                value = scaled[part, sheet]
                angle = 2.0 * math.pi * (sheet * freq % count) / count
                real = real + value * math.cos(angle)
                imag = imag - value * math.sin(angle)
            layered[freq // own, part, 0, freq % own] = real
            layered[freq // own, part, 1, freq % own] = imag
            if 0 < freq < sheets:
                other = count - freq
                layered[other // own, part, 0, other % own] = real
                layered[other // own, part, 1, other % own] = -imag
        return carry

    lax.fori_loop(0, parts, layer_part, 0)
    greet(tx, ty, ntx, nty)
    for part in range(parts):
        for step in range(1, ntx):
            over_tx(step, part).start()

    def transform(block, part):
        result = product(left_high[...], left_low[...], table_high[block], table_low[block])
        half = own * rows
        real = result[:half, :width] + result[half:, width:]
        imag = result[half:, :width] - result[:half, width:]
        return real.reshape(own, rows, width), imag.reshape(own, rows, width)

    def transform_part(part, carry):
        for step in range(1, ntx):
            over_tx(step, part).wait_recv()
        gathered[tx, part] = layered[tx, part]
        for source in range(ntx):
            high, low = split(gathered[source, part].reshape(2 * own * rows, width))
            left_high[:, source * width : (source + 1) * width] = high
            left_low[:, source * width : (source + 1) * width] = low

        def one(step, inner):
            block = lax.rem(ty + step, nty)
            real, imag = transform(block, part)
            blocks[block, part, :, :, :width] = real
            blocks[block, part, :, :, width:] = imag
            over_ty(step, part).start()
            return inner

        lax.fori_loop(1, nty, one, 0)
        real, imag = transform(ty, part)
        out[ty, part, :, :, :width] = real
        out[ty, part, :, :, width:] = imag
        return carry

    lax.fori_loop(0, parts, transform_part, 0)
    for part in range(parts):
        for step in range(1, ntx):
            over_tx(step, part).wait_send()
        for step in range(1, nty):
            over_ty(step, part).wait()


def backward_kernel(
    ntx, nty, arrived, tensor_hbm, fwd_high, fwd_low, back_high, back_low, x_high_hbm, x_low_hbm,
    layers, out, tensor, x_high, x_low, spectra, field, returned, left_high, left_low, partial,
    landed, local_sem, ty_send, ty_recv, tx_send, tx_recv,
):
    tx, ty = lax.axis_index("tx"), lax.axis_index("ty")
    parts, own, rows = arrived.shape[1:4]
    width = arrived.shape[4] // 2
    total = nty * rows
    sheets = out.shape[1]
    tx_sems, ty_sems = (tx_send, tx_recv), (ty_send, ty_recv)
    loads = [
        pltpu.make_async_copy(tensor_hbm, tensor, local_sem.at[0]),
        pltpu.make_async_copy(x_high_hbm, x_high, local_sem.at[1]),
        pltpu.make_async_copy(x_low_hbm, x_low, local_sem.at[2]),
    ]
    for load in loads:
        load.start()

    def over_ty(step, part):
        return send_over("ty", step, part, field, returned, ty_sems, ntx, nty)

    def over_tx(step, part):
        return send_over("tx", step, part, partial, landed, tx_sems, ntx, nty)

    def forward_rows(index, carry):
        part, freq = index // own, index % own
        high, low = split(arrived[:, part, freq].reshape(total, 2 * width))
        result = product(fwd_high[...], fwd_low[...], high, low)
        half = 2 * total
        spectra[part, freq, :, :width] = result[:half, :width] + result[half:, width:]
        spectra[part, freq, :, width:] = result[:half, width:] - result[half:, :width]
        return carry

    lax.fori_loop(0, parts * own, forward_rows, 0)
    greet(tx, ty, ntx, nty)
    loads[0].wait()
    for part in range(parts):

        def back_rows(freq, carry):
            sides = []
            for side in range(2):
                lanes = slice(side * width, (side + 1) * width)
                sides.append(
                    tensor[PAIRS[part][0], freq] * spectra[0, freq, :, lanes]
                    + tensor[PAIRS[part][1], freq] * spectra[1, freq, :, lanes]
                    + tensor[PAIRS[part][2], freq] * spectra[2, freq, :, lanes]
                )
            high, low = split(jnp.concatenate(sides, axis=1))
            result = product(back_high[...], back_low[...], high, low)
            real = result[:total, :width] - result[total:, width:]
            imag = result[:total, width:] + result[total:, :width]
            field[:, part, 0, freq] = real.reshape(nty, rows, width)
            field[:, part, 1, freq] = imag.reshape(nty, rows, width)
            return carry

        lax.fori_loop(0, own, back_rows, 0)
        for step in range(1, nty):
            over_ty(step, part).start()
        returned[ty, part] = field[ty, part]
    loads[1].wait()
    loads[2].wait()

    def transform(block):
        result = product(left_high[...], left_low[...], x_high[block], x_low[block])
        half = own * rows
        real = result[:half, :width] - result[half:, width:]
        imag = result[:half, width:] + result[half:, :width]
        real, imag = real.reshape(own, rows, width), imag.reshape(own, rows, width)
        values = []
        for sheet in range(sheets):
            value = jnp.zeros((rows, width), jnp.float32)
            for freq in range(own):
                value = value + layers[tx * own + freq, 2 * sheet] * real[freq]
                value = value - layers[tx * own + freq, 2 * sheet + 1] * imag[freq]
            values.append(value)
        return values

    def inverse_part(part, carry):
        for step in range(1, nty):
            over_ty(step, part).wait_recv()
        for source in range(nty):
            high, low = split(returned[source, part].reshape(2 * own * rows, width))
            left_high[:, source * width : (source + 1) * width] = high
            left_low[:, source * width : (source + 1) * width] = low

        def one(step, inner):
            block = lax.rem(tx + step, ntx)
            for sheet, value in enumerate(transform(block)):
                partial[block, part, sheet] = value
            over_tx(step, part).start()
            return inner

        lax.fori_loop(1, ntx, one, 0)
        for sheet, value in enumerate(transform(tx)):
            landed[tx, part, sheet] = value
        return carry

    lax.fori_loop(0, parts, inverse_part, 0)
    for part in range(parts):
        for step in range(1, ntx):
            over_tx(step, part).wait_recv()
        total_field = landed[0, part]
        for source in range(1, ntx):
            total_field = total_field + landed[source, part]
        out[part] = total_field
    for part in range(parts):
        for step in range(1, nty):
            over_ty(step, part).wait_send()
        for step in range(1, ntx):
            over_tx(step, part).wait_send()


def vmem():
    return pl.BlockSpec(memory_space=pltpu.VMEM)


def params(identity):
    return pltpu.CompilerParams(
        collective_id=identity, has_side_effects=True, vmem_limit_bytes=60 * 1024 * 1024
    )


def spectra_over_rows(scaled, ntx, nty):
    parts, sheets, rows, width = scaled.shape
    own = 2 * sheets // ntx
    high, low = halves(blocked_pair(angles(ntx * width, nty * width, 2 * ntx * width), width))
    lines = 2 * own * rows
    dma = pltpu.SemaphoreType.DMA
    return pl.pallas_call(
        functools.partial(forward_kernel, ntx, nty),
        out_shape=jax.ShapeDtypeStruct((nty, parts, own, rows, 2 * width), jnp.float32),
        in_specs=[vmem()] * 3,
        out_specs=vmem(),
        scratch_shapes=[
            pltpu.VMEM((ntx, parts, 2, own, rows, width), jnp.float32),
            pltpu.VMEM((ntx, parts, 2, own, rows, width), jnp.float32),
            pltpu.VMEM((lines, ntx * width), jnp.bfloat16),
            pltpu.VMEM((lines, ntx * width), jnp.bfloat16),
            pltpu.VMEM((nty, parts, own, rows, 2 * width), jnp.float32),
            dma((parts, ntx)),
            dma((parts, ntx)),
            dma((parts, nty)),
            dma((parts, nty)),
        ],
        compiler_params=params(0),
        name="forward_spectra",
    )(scaled, high, low)


def field_from_spectra(arrived, stray_tensor, sheets, ntx, nty):
    parts, own, rows = arrived.shape[1:4]
    width = arrived.shape[4] // 2
    total, columns = nty * rows, ntx * width
    count = 2 * sheets
    forward = angles(2 * total, total, 2 * total)
    forward = halves(np.concatenate([np.cos(forward), np.sin(forward)], axis=0))
    back = angles(total, 2 * total, 2 * total)
    back = halves(np.concatenate([np.cos(back), np.sin(back)], axis=0))
    x_table = halves(blocked_pair(angles(nty * width, columns, 2 * columns), width))
    turn = angles(count, sheets, count)
    scale = -1.0 / (count * 2 * total * 2 * columns)
    layers = np.stack([np.cos(turn), np.sin(turn)], axis=2).reshape(count, 2 * sheets) * scale
    lines = 2 * own * rows
    dma = pltpu.SemaphoreType.DMA
    anywhere = pl.BlockSpec(memory_space=pl.ANY)
    return pl.pallas_call(
        functools.partial(backward_kernel, ntx, nty),
        out_shape=jax.ShapeDtypeStruct((parts, sheets, rows, width), jnp.float32),
        in_specs=[vmem(), anywhere, vmem(), vmem(), vmem(), vmem(), anywhere, anywhere]
        + [pl.BlockSpec(memory_space=pltpu.SMEM)],
        out_specs=vmem(),
        scratch_shapes=[
            pltpu.VMEM(stray_tensor.shape, jnp.float32),
            pltpu.VMEM(x_table[0].shape, jnp.bfloat16),
            pltpu.VMEM(x_table[1].shape, jnp.bfloat16),
            pltpu.VMEM((parts, own, 2 * total, 2 * width), jnp.float32),
            pltpu.VMEM((nty, parts, 2, own, rows, width), jnp.float32),
            pltpu.VMEM((nty, parts, 2, own, rows, width), jnp.float32),
            pltpu.VMEM((lines, nty * width), jnp.bfloat16),
            pltpu.VMEM((lines, nty * width), jnp.bfloat16),
            pltpu.VMEM((ntx, parts, sheets, rows, width), jnp.float32),
            pltpu.VMEM((ntx, parts, sheets, rows, width), jnp.float32),
            dma((3,)),
            dma((parts, nty)),
            dma((parts, nty)),
            dma((parts, ntx)),
            dma((parts, ntx)),
        ],
        compiler_params=params(1),
        name="field_return",
    )(arrived, stray_tensor, *forward, *back, *x_table, layers.astype(np.float32))


def local(
    reduced_heat,
    substance_kind,
    moment_vector,
    stray_tensor,
    diffusivity_nodes,
    substance_factor,
    ordering_threshold,
    beam_transverse_spot,
    beam_downtrack_spot,
):
    sheet_indices, downtrack_indices, transverse_indices = reduced_heat.shape
    total_rows = downtrack_indices * lax.axis_size("ty")
    total_cols = transverse_indices * lax.axis_size("tx")
    row_base = lax.axis_index("ty") * downtrack_indices
    col_base = lax.axis_index("tx") * transverse_indices
    rotation_phase = reduced_heat - AMBIENT_HEAT
    site_multiplier = per_particle(substance_kind, substance_factor)
    row_ids = row_base + jnp.arange(downtrack_indices, dtype=jnp.int32)
    col_ids = col_base + jnp.arange(transverse_indices, dtype=jnp.int32)
    for sweep in range(SWEEPS):
        diffusivity = site_multiplier * lookup_diffusivity(
            rotation_phase + AMBIENT_HEAT, diffusivity_nodes
        )
        fields = jnp.stack([rotation_phase, diffusivity])
        along = extended(fields, (("tx", 3),), 1, True)
        across = extended(fields, (("ty", 2),), 1, False)
        neighbours = [
            (along[0, :, :, :-2], along[1, :, :, :-2]),
            (along[0, :, :, 2:], along[1, :, :, 2:]),
            (across[0, :, :-2], across[1, :, :-2]),
            (across[0, :, 2:], across[1, :, 2:]),
        ]
        heating = laser_heating(
            row_ids,
            col_ids,
            sheet_indices,
            beam_transverse_spot[sweep],
            beam_downtrack_spot[sweep],
            total_cols,
            0.5 * transverse_indices,
            1.0 * downtrack_indices,
        )
        rotation_phase = heat_update(rotation_phase, diffusivity, neighbours, heating)
    warmed_state = rotation_phase + AMBIENT_HEAT
    proportion = jax.nn.sigmoid(
        (per_particle(substance_kind, ordering_threshold) - warmed_state) / ORDERING_SPREAD
    )
    scaled = moment_vector * proportion[None]
    ntx, nty = lax.axis_size("tx"), lax.axis_size("ty")
    arrived = spectra_over_rows(scaled, ntx, nty)
    demag_field = field_from_spectra(arrived, stray_tensor, sheet_indices, ntx, nty)
    return (warmed_state, demag_field)


def solution(mesh):
    in_specs = (
        P(None, "ty", "tx"),
        P(None, "ty", "tx"),
        P(None, None, "ty", "tx"),
        P(None, "tx", None, "ty"),
        P(),
        P(),
        P(),
        P(),
        P(),
    )
    out_specs = (P(None, "ty", "tx"), P(None, None, "ty", "tx"))
    return jax.shard_map(local, mesh=mesh, in_specs=in_specs, out_specs=out_specs, check_vma=False)
```

time: 573 us -> 205 us (0.36)
  the two profiles are of different devices: /device:TPU:2 before, /device:TPU:9 now
where the time goes in v1:
time: 205 us
  Pallas kernels  128 us (62%)
  between operations  19.5 us (10%)
  waiting for transfers between devices  17 us (8%)
  other arithmetic  16.9 us (8%)
  starting transfers between devices  15.7 us (8%)
  local copies, waits for them, and re-layouts  7.13 us (3%)
    pallas_call x1, Pallas kernels, spectra_over_rows(): pl.pallas_call(functools.partial(forward_kernel, ntx, nty), out_shape=jax...  64.7 us
    pallas_call x1, Pallas kernels, field_from_spectra(): pl.pallas_call(functools.partial(backward_kernel, ntx, nty), out_shape=ja...  63.7 us
    ppermute x4, starting transfers between devices, extended(): before = lax.ppermute(last, axis, up)  10.7 us
    ppermute x4, waiting for transfers between devices, extended(): before = lax.ppermute(last, axis, up)  8.9 us
    mul x2, other arithmetic, local(): site_multiplier * lookup_diffusivity(rotation_phase + AMBIENT_HEAT, diffu...  8.63 us
    ppermute x4, waiting for transfers between devices, extended(): after = lax.ppermute(first, axis, down)  8.05 us
    ppermute x4, starting transfers between devices, extended(): after = lax.ppermute(first, axis, down)  5.02 us
  transfers between devices with their start and end apart: 8, of which 4 were waited for; matrix products, arithmetic and copies ran while one was open for 2% of the time, Pallas kernels for 0%

profile of v1, /device:TPU:9, one launch (start us, length us, event | category | flops | bytes accessed | tf_op | source)
XLA Modules:
  0.0 204.6 jit_solution(6069771530070251615)
XLA Ops:
  0.7 1.5 fusion.79
  2.1 1.9 fusion.80
  22.7 0.9 fusion.73
  23.7 4.6 %add_multiply_fusion.1 = (f32[8,32,128]{2,1,0:T(8,128)S(1)}, pred[8,32,128]{2,1,0:T(8,128)(4,1)S(1)}, pred[8,32,128]{2,1,0:T(8,128)(4,1)S(1)}, pred[8,32,128]{2,1,0:T(8,128)(4,1)S(1)}, pred[8,32,128]{2,1,0:T(8,128)(4,1)S(1)}) fusion(f32[8,32,128]{2,1,0:T(8,128)} %param.18, f32[]{:T(128)S(6)} %sub.297, f32[]{:T(128)S(6)} %sub.295, f32[]{:T(128)S(6)} %sub.293, ...), kind=kLoop, calls=%fused_computation.100 | loop fusion | flops 2850816 | bytes 524368 | tf_op jit(solution)/shard_map/mul | solution.py:441
  28.3 3.7 %collective-permute-start.2 = (f32[2,8,1,128]{3,2,1,0:T(1,128)S(1)}, f32[2,8,1,128]{3,2,1,0:T(1,128)S(1)}, u32[]{:S(2)}, u32[]{:S(2)}) collective-permute-start(f32[2,8,1,128]{3,2,1,0:T(1,128)S(1)} %get-tuple-element.17), channel_id=1, source_target_pairs={{0,1},{1,2},{2,3},{3,4},{4,5},{5,6},{6,7},{8,9},{9,10},{10,11},{11... | collective-permute-start | bytes 24584 | tf_op jit(solution)/shard_map/ppermute | solution.py:32
  32.0 1.9 collective-permute-start.3
  34.1 1.3 collective-permute-start
  36.9 0.7 fusion.78
  37.6 0.7 multiply_exponential_fusion
  38.3 1.2 multiply_exponential_fusion.1
  39.5 0.7 multiply_exponential_fusion.2
  40.2 2.3 %collective-permute-done = f32[2,8,32,1]{3,2,1,0:T(8,128)S(1)} collective-permute-done((f32[2,8,32,1]{3,2,1,0:T(8,128)S(1)}, f32[2,8,32,1]{3,2,1,0:T(8,128)S(1)}, u32[]{:S(2)}, u32[]{:S(2)}) %collective-permute-start) | collective-permute-done | bytes 2080 | tf_op jit(solution)/shard_map/ppermute | solution.py:32
  42.5 4.6 %collective-permute-done.1 = f32[2,8,32,1]{3,2,1,0:T(8,128)S(1)} collective-permute-done((f32[2,8,32,1]{3,2,1,0:T(8,128)S(1)}, f32[2,8,32,1]{3,2,1,0:T(8,128)S(1)}, u32[]{:S(2)}, u32[]{:S(2)}) %collective-permute-start.1) | collective-permute-done | bytes 2080 | tf_op jit(solution)/shard_map/ppermute | solution.py:33
  47.2 4.0 %add_multiply_fusion = (f32[8,32,128]{2,1,0:T(8,128)S(1)}, f32[8,32,128]{2,1,0:T(8,128)S(1)}) fusion(pred[8,32,128]{2,1,0:T(8,128)(4,1)S(1)} %get-tuple-element.10, pred[8,32,128]{2,1,0:T(8,128)(4,1)S(1)} %get-tuple-element.9, pred[8,32,128]{2,1,0:T(8,128)(4,1)S(1)} %get-tuple-element.8, pred[8,32,128]{2,1,0:T(8,128)(4,1)S(1)} %get-tuple-element.7, ...), kind=kLoop, calls=%fused_computation.99 | loop fusion | flops 4128768 | bytes 1054288 | tf_op jit(solution)/shard_map/mul | solution.py:441
  51.3 5.2 %collective-permute-start.6 = (f32[2,8,1,128]{3,2,1,0:T(1,128)S(1)}, f32[2,8,1,128]{3,2,1,0:T(1,128)S(1)}, u32[]{:S(2)}, u32[]{:S(2)}) collective-permute-start(f32[2,8,1,128]{3,2,1,0:T(1,128)S(1)} %get-tuple-element.13), channel_id=1, source_target_pairs={{0,1},{1,2},{2,3},{3,4},{4,5},{5,6},{6,7},{8,9},{9,10},{10,11},{11... | collective-permute-start | bytes 24584 | tf_op jit(solution)/shard_map/ppermute | solution.py:32
  56.5 1.9 collective-permute-start.7
  59.0 1.0 collective-permute-start.5
  60.0 6.6 %collective-permute-done.4 = f32[2,8,32,1]{3,2,1,0:T(8,128)S(1)} collective-permute-done((f32[2,8,32,1]{3,2,1,0:T(8,128)S(1)}, f32[2,8,32,1]{3,2,1,0:T(8,128)S(1)}, u32[]{:S(2)}, u32[]{:S(2)}) %collective-permute-start.4) | collective-permute-done | bytes 2080 | tf_op jit(solution)/shard_map/ppermute | solution.py:32
  66.6 3.4 %collective-permute-done.5 = f32[2,8,32,1]{3,2,1,0:T(8,128)S(1)} collective-permute-done((f32[2,8,32,1]{3,2,1,0:T(8,128)S(1)}, f32[2,8,32,1]{3,2,1,0:T(8,128)S(1)}, u32[]{:S(2)}, u32[]{:S(2)}) %collective-permute-start.5) | collective-permute-done | bytes 2080 | tf_op jit(solution)/shard_map/ppermute | solution.py:33
  70.0 3.6 %add_divide_fusion = (f32[8,32,128]{2,1,0:T(8,128)S(1)}, f32[8,32,128]{2,1,0:T(8,128)}) fusion(pred[8,32,128]{2,1,0:T(8,128)(4,1)S(1)} %get-tuple-element.10, pred[8,32,128]{2,1,0:T(8,128)(4,1)S(1)} %get-tuple-element.9, pred[8,32,128]{2,1,0:T(8,128)(4,1)S(1)} %get-tuple-element.8, pred[8,32,128]{2,1,0:T(8,128)(4,1)S(1)} %get-tuple-element.7, f32[]{:T(128)} %bitcast.47, ...), kind=kLoop, calls=%fused_computation.98 | loop fusion | flops 1802240 | bytes 1054224 | tf_op jit(solution)/shard_map/div | solution.py:465
  73.6 0.8 broadcast_multiply_fusion.scaled
  74.4 64.7 %forward_spectra.1.arrived = f32[8,3,4,32,256]{4,3,2,1,0:T(8,128)} custom-call(f32[3,8,32,128]{3,2,1,0:T(8,128)} %broadcast_multiply_fusion.scaled, bf16[8,512,256]{2,1,0:T(8,128)(2,1)} %constant.224.clone.table_high, bf16[8,512,256]{2,1,0:T(8,128)(2,1)} %constant.225.clone.table_low), custom_call_target="tpu_custom_call" | custom-call | tf_op jit(solution)/shard_map/forward_spectra/pallas_call | solution.py:355
  139.1 63.7 %field_return.1 = f32[3,8,32,128]{3,2,1,0:T(8,128)} custom-call(f32[8,3,4,32,256]{4,3,2,1,0:T(8,128)} %forward_spectra.1.arrived, f32[6,4,512,128]{3,2,1,0:T(8,128)} %tensor_hbm.1, bf16[1024,256]{1,0:T(8,128)(2,1)} %constant.226.clone.fwd_high, bf16[1024,256]{1,0:T(8,128)(2,1)} %constant.227.clone.fwd_low, bf16[512,512]{1,0:T(8,128)(2,1)} %constant.228.clone.back_high, ...), custom_call_target="tpu_custom_call" | custom-call | tf_op jit(solution)/shard_map/field_return/pallas_call | solution.py:392
  202.8 1.8 copy.21
  (26 shorter events, 2.4 us)
Async XLA Ops:
  0.6 46.5 %copy-start = (f32[8,32,128]{2,1,0:T(8,128)S(1)}, f32[8,32,128]{2,1,0:T(8,128)}, u32[]{:S(2)}) copy-start(f32[8,32,128]{2,1,0:T(8,128)} %param.18) | copy-start | bytes 393220
  0.6 35.0 %copy-start.3 = (s32[2]{0:T(128)S(1)}, s32[2]{0:T(128)}, u32[]{:S(2)}) copy-start(s32[2]{0:T(128)} %param.25) | copy-start | bytes 28
  0.7 35.6 %copy-start.4 = (s32[2]{0:T(128)S(1)}, s32[2]{0:T(128)}, u32[]{:S(2)}) copy-start(s32[2]{0:T(128)} %param.26) | copy-start | bytes 28
  0.7 36.2 %copy-start.2 = (f32[4]{0:T(128)S(1)}, f32[4]{0:T(128)}, u32[]{:S(2)}) copy-start(f32[4]{0:T(128)} %param.24) | copy-start | bytes 52
  28.3 18.8 %collective-permute-start.2 = (f32[2,8,1,128]{3,2,1,0:T(1,128)S(1)}, f32[2,8,1,128]{3,2,1,0:T(1,128)S(1)}, u32[]{:S(2)}, u32[]{:S(2)}) collective-permute-start(f32[2,8,1,128]{3,2,1,0:T(1,128)S(1)} %get-tuple-element.17), channel_id=1, source_target_pairs={{0,1},{1,2},{2,3},{3,4},{4,5},{5,6},{6,7},{8,9},{9,10},{10,11},{11... | collective-permute-start | bytes 24584 | tf_op jit(solution)/shard_map/ppermute | solution.py:32
  32.0 15.1 %collective-permute-start.3 = (f32[2,8,1,128]{3,2,1,0:T(1,128)S(1)}, f32[2,8,1,128]{3,2,1,0:T(1,128)S(1)}, u32[]{:S(2)}, u32[]{:S(2)}) collective-permute-start(f32[2,8,1,128]{3,2,1,0:T(1,128)S(1)} %get-tuple-element.18), channel_id=1, source_target_pairs={{1,0},{2,1},{3,2},{4,3},{5,4},{6,5},{7,6},{9,8},{10,9},{11,10},{12... | collective-permute-start | bytes 24584 | tf_op jit(solution)/shard_map/ppermute | solution.py:33
  34.1 8.4 %collective-permute-start = (f32[2,8,32,1]{3,2,1,0:T(8,128)S(1)}, f32[2,8,32,1]{3,2,1,0:T(8,128)S(1)}, u32[]{:S(2)}, u32[]{:S(2)}) collective-permute-start(f32[2,8,32,1]{3,2,1,0:T(8,128)S(1)} %get-tuple-element.15), channel_id=1, source_target_pairs={{0,8},{8,16},{16,24},{24,0},{1,9},{9,17},{17,25},{25,1},{2,10},{10... | collective-permute-start | bytes 6152 | tf_op jit(solution)/shard_map/ppermute | solution.py:32
  35.4 11.7 %collective-permute-start.1 = (f32[2,8,32,1]{3,2,1,0:T(8,128)S(1)}, f32[2,8,32,1]{3,2,1,0:T(8,128)S(1)}, u32[]{:S(2)}, u32[]{:S(2)}) collective-permute-start(f32[2,8,32,1]{3,2,1,0:T(8,128)S(1)} %get-tuple-element.16), channel_id=1, source_target_pairs={{8,0},{16,8},{24,16},{0,24},{9,1},{17,9},{25,17},{1,25},{10,2},{18... | collective-permute-start | bytes 6152 | tf_op jit(solution)/shard_map/ppermute | solution.py:33
  47.2 26.4 %copy-start.1 = (f32[3,8,32,128]{3,2,1,0:T(8,128)S(1)}, f32[3,8,32,128]{3,2,1,0:T(8,128)}, u32[]{:S(2)}) copy-start(f32[3,8,32,128]{3,2,1,0:T(8,128)} %param.20) | copy-start | bytes 1179652
  51.3 18.7 %collective-permute-start.6 = (f32[2,8,1,128]{3,2,1,0:T(1,128)S(1)}, f32[2,8,1,128]{3,2,1,0:T(1,128)S(1)}, u32[]{:S(2)}, u32[]{:S(2)}) collective-permute-start(f32[2,8,1,128]{3,2,1,0:T(1,128)S(1)} %get-tuple-element.13), channel_id=1, source_target_pairs={{0,1},{1,2},{2,3},{3,4},{4,5},{5,6},{6,7},{8,9},{9,10},{10,11},{11... | collective-permute-start | bytes 24584 | tf_op jit(solution)/shard_map/ppermute | solution.py:32
  56.5 13.5 %collective-permute-start.7 = (f32[2,8,1,128]{3,2,1,0:T(1,128)S(1)}, f32[2,8,1,128]{3,2,1,0:T(1,128)S(1)}, u32[]{:S(2)}, u32[]{:S(2)}) collective-permute-start(f32[2,8,1,128]{3,2,1,0:T(1,128)S(1)} %get-tuple-element.14), channel_id=1, source_target_pairs={{1,0},{2,1},{3,2},{4,3},{5,4},{6,5},{7,6},{9,8},{10,9},{11,10},{12... | collective-permute-start | bytes 24584 | tf_op jit(solution)/shard_map/ppermute | solution.py:33
  58.4 8.1 %collective-permute-start.4 = (f32[2,8,32,1]{3,2,1,0:T(8,128)S(1)}, f32[2,8,32,1]{3,2,1,0:T(8,128)S(1)}, u32[]{:S(2)}, u32[]{:S(2)}) collective-permute-start(f32[2,8,32,1]{3,2,1,0:T(8,128)S(1)} %get-tuple-element.11), channel_id=1, source_target_pairs={{0,8},{8,16},{16,24},{24,0},{1,9},{9,17},{17,25},{25,1},{2,10},{10... | collective-permute-start | bytes 6152 | tf_op jit(solution)/shard_map/ppermute | solution.py:32
  59.0 11.0 %collective-permute-start.5 = (f32[2,8,32,1]{3,2,1,0:T(8,128)S(1)}, f32[2,8,32,1]{3,2,1,0:T(8,128)S(1)}, u32[]{:S(2)}, u32[]{:S(2)}) collective-permute-start(f32[2,8,32,1]{3,2,1,0:T(8,128)S(1)} %get-tuple-element.12), channel_id=1, source_target_pairs={{8,0},{16,8},{24,16},{0,24},{9,1},{17,9},{25,17},{1,25},{10,2},{18... | collective-permute-start | bytes 6152 | tf_op jit(solution)/shard_map/ppermute | solution.py:33

commit v2 on v1

--- a/solution.py
+++ b/solution.py
@@ -20,65 +20,6 @@
 ORDERING_SPREAD = 0.08
 TABLE_LOW = 0.2
 TABLE_SPAN = 1.6
-
-
-def extended(value, sides, width, wrap):
-    for axis, dim in sides:
-        count, length = (lax.axis_size(axis), value.shape[dim])
-        up = [(i, (i + 1) % count) for i in range(count if wrap else count - 1)]
-        down = [(j, i) for i, j in up]
-        last = lax.slice_in_dim(value, length - width, length, axis=dim)
-        first = lax.slice_in_dim(value, 0, width, axis=dim)
-        before = lax.ppermute(last, axis, up)
-        after = lax.ppermute(first, axis, down)
-        value = jnp.concatenate([before, value, after], axis=dim)
-    return value
-
-
-def lookup_diffusivity(absolute, diffusivity_nodes):
-    nodes = diffusivity_nodes.shape[0]
-    spacing = TABLE_SPAN / (nodes - 1)
-    total = jnp.zeros_like(absolute) + diffusivity_nodes[0]
-    for index in range(nodes - 1):
-        start_node = TABLE_LOW + index * spacing
-        total = total + (diffusivity_nodes[index + 1] - diffusivity_nodes[index]) * jnp.clip(
-            (absolute - start_node) / spacing, 0.0, 1.0
-        )
-    return total
-
-
-def per_particle(substance_kind, values):
-    result = jnp.zeros(substance_kind.shape, jnp.float32)
-    for grain in range(values.shape[0]):
-        result = result + jnp.where(substance_kind == grain, values[grain], 0.0)
-    return result
-
-
-def laser_heating(
-    row_ids, col_ids, sheet_indices, spot_row, spot_col, total_cols, col_width, row_width
-):
-    along = ((col_ids - spot_col + total_cols // 2) % total_cols - total_cols // 2).astype(
-        jnp.float32
-    ) / col_width
-    across = (row_ids - spot_row).astype(jnp.float32) / row_width
-    col_factor = jnp.exp(-0.5 * along * along)
-    row_factor = jnp.exp(-0.5 * across * across)
-    layer_factor = jnp.exp(-jnp.arange(sheet_indices, dtype=jnp.float32) / LASER_DEPTH)
-    return layer_factor[:, None, None] * row_factor[None, :, None] * col_factor[None, None, :]
-
-
-def heat_update(center, diffusivity, neighbours, heating):
-    flux = jnp.zeros_like(center)
-    for other_temp, other_cond in neighbours:
-        flux = flux + 0.5 * (diffusivity + other_cond) * (other_temp - center)
-    vertical = 0.5 * (diffusivity[1:] + diffusivity[:-1]) * (center[1:] - center[:-1])
-    zero_layer = jnp.zeros_like(center[:1])
-    flux = (
-        flux
-        + jnp.concatenate([vertical, zero_layer], 0)
-        - jnp.concatenate([zero_layer, vertical], 0)
-    )
-    return center + STEP_RATE * (flux + LASER_POWER * heating)
 
 
 MESH = pl.DeviceIdType.MESH
@@ -146,12 +87,128 @@
     )
 
 
-def forward_kernel(
-    ntx, nty, scaled, table_high, table_low, out, layered, gathered, left_high, left_low, blocks,
-    tx_send, tx_recv, ty_send, ty_recv,
+def conductivity(absolute, multiplier, nodes):
+    count = nodes.shape[0]
+    spacing = TABLE_SPAN / (count - 1)
+    total = jnp.zeros_like(absolute) + nodes[0]
+    for index in range(count - 1):
+        place = (absolute - (TABLE_LOW + index * spacing)) * (1.0 / spacing)
+        total = total + (nodes[index + 1] - nodes[index]) * jnp.clip(place, 0.0, 1.0)
+    return multiplier * total
+
+
+def of_kind(kind, values):
+    result = jnp.zeros(kind.shape, jnp.float32)
+    for grain in range(values.shape[0]):
+        result = result + jnp.where(kind == grain, values[grain], 0.0)
+    return result
+
+
+def laser_plane(rows, width, tx, ty, ntx, row_spot, col_spot):
+    total = ntx * width
+    row_ids = lax.broadcasted_iota(jnp.int32, (rows, width), 0) + ty * rows
+    col_ids = lax.broadcasted_iota(jnp.int32, (rows, width), 1) + tx * width
+    along = col_ids - col_spot + total // 2
+    along = jnp.where(along < 0, along + total, along)
+    along = jnp.where(along >= total, along - total, along) - total // 2
+    along = along.astype(jnp.float32) * (1.0 / (0.5 * width))
+    across = (row_ids - row_spot).astype(jnp.float32) * (1.0 / rows)
+    return jnp.exp(-0.5 * across * across) * jnp.exp(-0.5 * along * along)
+
+
+def heat_sweeps(
+    ntx, nty, heat, kind, nodes, factor, row_spots, col_spots, rows_out, rows_in, cols_out, cols_in,
+    edge_send, edge_recv,
 ):
     tx, ty = lax.axis_index("tx"), lax.axis_index("ty")
-    parts, sheets, rows, width = scaled.shape
+    sheets, rows, width = heat.shape
+    flat, cube = (sheets * rows, width), (sheets, rows, width)
+    lane = lax.broadcasted_iota(jnp.int32, cube, 2)
+    line = lax.broadcasted_iota(jnp.int32, cube, 1)
+    theta = heat[...] - AMBIENT_HEAT
+    multiplier = of_kind(kind[...], factor)
+    started = []
+    for sweep in range(SWEEPS):
+        cond = conductivity(theta + AMBIENT_HEAT, multiplier, nodes)
+        pair = (theta, cond)
+        for place, value in enumerate(pair):
+            rows_out[sweep, 0, place] = value[:, 0, :]
+            rows_out[sweep, 1, place] = value[:, rows - 1, :]
+            turned = value.reshape(flat).T
+            cols_out[sweep, 0, place : place + 1] = turned[:1]
+            cols_out[sweep, 1, place : place + 1] = turned[width - 1 :]
+        copies = []
+        for side, shift in enumerate((-1, 1)):
+            targets = (
+                (cols_out, cols_in, (lax.rem(tx + shift + ntx, ntx), ty)),
+                (rows_out, rows_in, (tx, lax.rem(ty + shift + nty, nty))),
+            )
+            for axis, (source, target, device) in enumerate(targets):
+                copy = pltpu.make_async_remote_copy(
+                    src_ref=source.at[sweep, side],
+                    dst_ref=target.at[sweep, side],
+                    send_sem=edge_send.at[sweep, side, axis],
+                    recv_sem=edge_recv.at[sweep, side, axis],
+                    device_id=device,
+                    device_id_type=MESH,
+                )
+                copy.start()
+                copies.append(copy)
+        started += copies
+        plane = laser_plane(rows, width, tx, ty, ntx, row_spots[sweep], col_spots[sweep])
+        heating = jnp.stack([plane * math.exp(-sheet / LASER_DEPTH) for sheet in range(sheets)])
+        vertical = 0.5 * (cond[1:] + cond[:-1]) * (theta[1:] - theta[:-1])
+        zero_layer = jnp.zeros_like(theta[:1])
+        flux = jnp.concatenate([vertical, zero_layer], 0) - jnp.concatenate(
+            [zero_layer, vertical], 0
+        )
+        for copy in copies:
+            copy.wait_recv()
+        for side, shift in enumerate((-1, 1)):
+            turned = cols_in[sweep, side].T
+            edge = 0 if shift == 1 else width - 1
+            other = []
+            for place, value in enumerate(pair):
+                moved = pltpu.roll(value.reshape(flat), shift % width, 1).reshape(cube)
+                column = turned[:, place : place + 1].reshape(sheets, rows, 1)
+                other.append(jnp.where(lane == edge, column, moved))
+            flux = flux + 0.5 * (cond + other[1]) * (other[0] - theta)
+            edge = 0 if shift == 1 else rows - 1
+            inside = ty > 0 if shift == 1 else ty < nty - 1
+            other = []
+            for place, value in enumerate(pair):
+                moved = pltpu.roll(value.reshape(flat), shift % flat[0], 0).reshape(cube)
+                row = jnp.where(inside, rows_in[sweep, side, place], 0.0)
+                other.append(jnp.where(line == edge, row[:, None, :], moved))
+            flux = flux + 0.5 * (cond + other[1]) * (other[0] - theta)
+        theta = theta + STEP_RATE * (flux + LASER_POWER * heating)
+    return theta + AMBIENT_HEAT, started
+
+
+def edge_scratch(sheets, rows, width):
+    edge_rows = pltpu.VMEM((SWEEPS, 2, 2, sheets, width), jnp.float32)
+    edge_cols = pltpu.VMEM((SWEEPS, 2, 8, sheets * rows), jnp.float32)
+    sems = pltpu.SemaphoreType.DMA((SWEEPS, 2, 2))
+    return [edge_rows, edge_rows, edge_cols, edge_cols, sems, sems]
+
+
+def forward_kernel(
+    ntx, nty, heat, kind, moment, nodes, factor, threshold, row_spots, col_spots, table_high,
+    table_low, warmed, out, proportion, layered, gathered, left_high, left_low, blocks, rows_out,
+    rows_in, cols_out, cols_in, edge_send, edge_recv, tx_send, tx_recv, ty_send, ty_recv,
+):
+    tx, ty = lax.axis_index("tx"), lax.axis_index("ty")
+    parts, sheets, rows, width = moment.shape
+    greet(tx, ty, ntx, nty)
+    cols_out[...] = jnp.zeros_like(cols_out)
+    state, edges = heat_sweeps(
+        ntx, nty, heat, kind, nodes, factor, row_spots, col_spots, rows_out, rows_in, cols_out,
+        cols_in, edge_send, edge_recv,
+    )
+    warmed[...] = state
+    proportion[...] = jax.nn.sigmoid(
+        (of_kind(kind[...], threshold) - state) * (1.0 / ORDERING_SPREAD)
+    )
     count = 2 * sheets
     own = count // ntx
     tx_sems, ty_sems = (tx_send, tx_recv), (ty_send, ty_recv)
@@ -167,7 +224,7 @@
             real = jnp.zeros((rows, width), jnp.float32)
             imag = jnp.zeros((rows, width), jnp.float32)
             for sheet in range(sheets):
-                value = scaled[part, sheet]
+                value = moment[part, sheet] * proportion[sheet]
                 angle = 2.0 * math.pi * (sheet * freq % count) / count
                 real = real + value * math.cos(angle)
                 imag = imag - value * math.sin(angle)
@@ -179,9 +236,8 @@
                 layered[other // own, part, 1, other % own] = -imag
         return carry
 
-    lax.fori_loop(0, parts, layer_part, 0)
-    greet(tx, ty, ntx, nty)
     for part in range(parts):
+        layer_part(part, 0)
         for step in range(1, ntx):
             over_tx(step, part).start()
 
@@ -216,6 +272,8 @@
         return carry
 
     lax.fori_loop(0, parts, transform_part, 0)
+    for edge in edges:
+        edge.wait_send()
     for part in range(parts):
         for step in range(1, ntx):
             over_tx(step, part).wait_send()
@@ -346,23 +404,30 @@
     )
 
 
-def spectra_over_rows(scaled, ntx, nty):
-    parts, sheets, rows, width = scaled.shape
+def spectra_over_rows(heat, kind, moment, scalars, ntx, nty):
+    parts, sheets, rows, width = moment.shape
     own = 2 * sheets // ntx
     high, low = halves(blocked_pair(angles(ntx * width, nty * width, 2 * ntx * width), width))
     lines = 2 * own * rows
     dma = pltpu.SemaphoreType.DMA
     return pl.pallas_call(
         functools.partial(forward_kernel, ntx, nty),
-        out_shape=jax.ShapeDtypeStruct((nty, parts, own, rows, 2 * width), jnp.float32),
-        in_specs=[vmem()] * 3,
-        out_specs=vmem(),
+        out_shape=(
+            jax.ShapeDtypeStruct(heat.shape, jnp.float32),
+            jax.ShapeDtypeStruct((nty, parts, own, rows, 2 * width), jnp.float32),
+        ),
+        in_specs=[vmem()] * 3
+        + [pl.BlockSpec(memory_space=pltpu.SMEM)] * len(scalars)
+        + [vmem()] * 2,
+        out_specs=(vmem(), vmem()),
         scratch_shapes=[
+            pltpu.VMEM((sheets, rows, width), jnp.float32),
             pltpu.VMEM((ntx, parts, 2, own, rows, width), jnp.float32),
             pltpu.VMEM((ntx, parts, 2, own, rows, width), jnp.float32),
             pltpu.VMEM((lines, ntx * width), jnp.bfloat16),
             pltpu.VMEM((lines, ntx * width), jnp.bfloat16),
             pltpu.VMEM((nty, parts, own, rows, 2 * width), jnp.float32),
+            *edge_scratch(sheets, rows, width),
             dma((parts, ntx)),
             dma((parts, ntx)),
             dma((parts, nty)),
@@ -370,7 +435,7 @@
         ],
         compiler_params=params(0),
         name="forward_spectra",
-    )(scaled, high, low)
+    )(heat, kind, moment, *scalars, high, low)
 
 
 def field_from_spectra(arrived, stray_tensor, sheets, ntx, nty):
@@ -428,47 +493,18 @@
     beam_transverse_spot,
     beam_downtrack_spot,
 ):
-    sheet_indices, downtrack_indices, transverse_indices = reduced_heat.shape
-    total_rows = downtrack_indices * lax.axis_size("ty")
-    total_cols = transverse_indices * lax.axis_size("tx")
-    row_base = lax.axis_index("ty") * downtrack_indices
-    col_base = lax.axis_index("tx") * transverse_indices
-    rotation_phase = reduced_heat - AMBIENT_HEAT
-    site_multiplier = per_particle(substance_kind, substance_factor)
-    row_ids = row_base + jnp.arange(downtrack_indices, dtype=jnp.int32)
-    col_ids = col_base + jnp.arange(transverse_indices, dtype=jnp.int32)
-    for sweep in range(SWEEPS):
-        diffusivity = site_multiplier * lookup_diffusivity(
-            rotation_phase + AMBIENT_HEAT, diffusivity_nodes
-        )
-        fields = jnp.stack([rotation_phase, diffusivity])
-        along = extended(fields, (("tx", 3),), 1, True)
-        across = extended(fields, (("ty", 2),), 1, False)
-        neighbours = [
-            (along[0, :, :, :-2], along[1, :, :, :-2]),
-            (along[0, :, :, 2:], along[1, :, :, 2:]),
-            (across[0, :, :-2], across[1, :, :-2]),
-            (across[0, :, 2:], across[1, :, 2:]),
-        ]
-        heating = laser_heating(
-            row_ids,
-            col_ids,
-            sheet_indices,
-            beam_transverse_spot[sweep],
-            beam_downtrack_spot[sweep],
-            total_cols,
-            0.5 * transverse_indices,
-            1.0 * downtrack_indices,
-        )
-        rotation_phase = heat_update(rotation_phase, diffusivity, neighbours, heating)
-    warmed_state = rotation_phase + AMBIENT_HEAT
-    proportion = jax.nn.sigmoid(
-        (per_particle(substance_kind, ordering_threshold) - warmed_state) / ORDERING_SPREAD
-    )
-    scaled = moment_vector * proportion[None]
     ntx, nty = lax.axis_size("tx"), lax.axis_size("ty")
-    arrived = spectra_over_rows(scaled, ntx, nty)
-    demag_field = field_from_spectra(arrived, stray_tensor, sheet_indices, ntx, nty)
+    scalars = (
+        diffusivity_nodes,
+        substance_factor,
+        ordering_threshold,
+        beam_transverse_spot,
+        beam_downtrack_spot,
+    )
+    warmed_state, arrived = spectra_over_rows(
+        reduced_heat, substance_kind, moment_vector, scalars, ntx, nty
+    )
+    demag_field = field_from_spectra(arrived, stray_tensor, reduced_heat.shape[0], ntx, nty)
     return (warmed_state, demag_field)
 
 

time: 205 us -> 137 us (0.67)
  between operations: 19.5 us -> 0.66 us
  waiting for transfers between devices: 17 us -> 0 us
  other arithmetic: 16.9 us -> 0 us
  starting transfers between devices: 15.7 us -> 0 us
  Pallas kernels: 128 us -> 134 us
  local copies, waits for them, and re-layouts: 7.13 us -> 2.43 us
    ppermute x8 -> x0, waiting for transfers between devices: 17 us -> none  [the longest x4 8.9 us: extended(): before = lax.ppermute(last, axis, up)]
    ppermute x8 -> x0, starting transfers between devices: 15.7 us -> none  [the longest x4 10.7 us: extended(): before = lax.ppermute(last, axis, up)]
    mul x6 -> x0, other arithmetic: 9.53 us -> none  [the longest x2 8.63 us: local(): site_multiplier * lookup_diffusivity(rotation_phase + AMBIENT_HEAT, diffu...]
    pallas_call x1, Pallas kernels: 64.7 us -> 70.4 us  [spectra_over_rows(): pl.pallas_call(functools.partial(forward_kernel, ntx, nty), out_shape=(ja...]
    slice x5 -> x0, local copies, waits for them, and re-layouts: 5.34 us -> none  [the longest x2 2.13 us: per_particle(): result = result + jnp.where(substance_kind == grain, values[grain], 0.0)]
    div x1 -> x0, other arithmetic: 3.55 us -> none  [local(): jax.nn.sigmoid((per_particle(substance_kind, ordering_threshold) - warmed...]
    exp x4 -> x0, other arithmetic: 2.57 us -> none  [the longest x2 1.38 us: laser_heating(): col_factor = jnp.exp(-0.5 * along * along)]
  transfers between devices with their start and end apart: 8 -> 0, of which waited for: 4 -> 0; matrix products, arithmetic and copies ran while one was open for 2% -> 0% of each run, Pallas kernels for 0% -> 0%
where the time goes in v2:
time: 137 us
  Pallas kernels  134 us (98%)
  local copies, waits for them, and re-layouts  2.43 us (2%)
    pallas_call x1, Pallas kernels, spectra_over_rows(): pl.pallas_call(functools.partial(forward_kernel, ntx, nty), out_shape=(ja...  70.4 us
    pallas_call x1, Pallas kernels, field_from_spectra(): pl.pallas_call(functools.partial(backward_kernel, ntx, nty), out_shape=ja...  63.3 us

profile of v2, /device:TPU:9, one launch (start us, length us, event | category | flops | bytes accessed | tf_op | source)
XLA Modules:
  0.0 136.8 jit_solution(13287996351380722694)
XLA Ops:
  0.6 70.4 %forward_spectra.1 = (f32[8,32,128]{2,1,0:T(8,128)}, f32[8,3,4,32,256]{4,3,2,1,0:T(8,128)}) custom-call(f32[8,32,128]{2,1,0:T(8,128)} %heat.1, s32[8,32,128]{2,1,0:T(8,128)} %kind.1, f32[3,8,32,128]{3,2,1,0:T(8,128)} %moment.1, f32[16]{0:T(128)} %nodes.1, f32[4]{0:T(128)} %factor.1, f32[4]{0:T(128)} %threshold.1, s32[2]{0:T(128)} %row_spots.1, s32[2]{0:T(128)} %col_spots.1, ...), custom_call_target="tpu_custom_call" | custom-call | tf_op jit(solution)/shard_map/forward_spectra/pallas_call | solution.py:413
  71.0 0.0 copy-start
  71.0 63.3 %field_return.1 = f32[3,8,32,128]{3,2,1,0:T(8,128)} custom-call(f32[8,3,4,32,256]{4,3,2,1,0:T(8,128)} %get-tuple-element.5.arrived, f32[6,4,512,128]{3,2,1,0:T(8,128)} %tensor_hbm.1, bf16[1024,256]{1,0:T(8,128)(2,1)} %constant.20.clone.fwd_high, bf16[1024,256]{1,0:T(8,128)(2,1)} %constant.21.clone.fwd_low, bf16[512,512]{1,0:T(8,128)(2,1)} %constant.22.clone.back_high, ...), custom_call_target="tpu_custom_call" | custom-call | tf_op jit(solution)/shard_map/field_return/pallas_call | solution.py:457
  134.3 0.0 copy-done
  134.3 0.7 copy.22
  135.0 1.8 %copy.23 = f32[3,8,32,128]{3,2,1,0:T(8,128)} copy(f32[3,8,32,128]{3,2,1,0:T(8,128)} %field_return.1) | data formatting | bytes 786432
Async XLA Ops:
  71.0 63.3 %copy-start = (f32[8,32,128]{2,1,0:T(8,128)S(1)}, f32[8,32,128]{2,1,0:T(8,128)}, u32[]{:S(2)}) copy-start(f32[8,32,128]{2,1,0:T(8,128)} %get-tuple-element.8) | copy-start | bytes 393220

commit v3 on v2

--- a/solution.py
+++ b/solution.py
@@ -23,6 +23,8 @@
 
 
 MESH = pl.DeviceIdType.MESH
+AHEAD = 2
+TABLE_BYTES = 16 * 1024 * 1024
 PAIRS = ((0, 3, 4), (3, 1, 5), (4, 5, 2))
 
 
@@ -482,6 +484,286 @@
     )(arrived, stray_tensor, *forward, *back, *x_table, layers.astype(np.float32))
 
 
+def whole_kernel(
+    ntx, nty, heat, kind, moment, nodes, factor, threshold, row_spots, col_spots, fwd_high, fwd_low,
+    back_high, back_low, tensor_hbm, to_high_hbm, to_low_hbm, from_high_hbm, from_low_hbm,
+    warmed, out, proportion, layered, gathered, blocks, arrived, spectra, field, returned, partial,
+    landed, tensor, to_high, to_low, from_high, from_low, along_high, along_low, inverse_high,
+    inverse_low, rows_out, rows_in, cols_out, cols_in, edge_send, edge_recv, local_sem, tx_send,
+    tx_recv, ty_send, ty_recv, ty_back_send, ty_back_recv, tx_back_send, tx_back_recv,
+):
+    tx, ty = lax.axis_index("tx"), lax.axis_index("ty")
+    parts, sheets, rows, width = moment.shape
+    count = 2 * sheets
+    own = count // ntx
+    total = nty * rows
+    half = parts * rows
+    loads = [
+        pltpu.make_async_copy(source, target, local_sem.at[index])
+        for index, (source, target) in enumerate(
+            (
+                (to_high_hbm, to_high),
+                (to_low_hbm, to_low),
+                (tensor_hbm, tensor),
+                (from_high_hbm, from_high),
+                (from_low_hbm, from_low),
+            )
+        )
+    ]
+    for load in loads:
+        load.start()
+
+    def tx_copy(step, freq):
+        sems = (tx_send, tx_recv)
+        return send_over("tx", step, freq, layered, gathered, sems, ntx, nty)
+
+    def ty_copy(step, freq):
+        return send_over("ty", step, freq, blocks, arrived, (ty_send, ty_recv), ntx, nty)
+
+    def ty_return(step, freq):
+        sems = (ty_back_send, ty_back_recv)
+        return send_over("ty", step, freq, field, returned, sems, ntx, nty)
+
+    def tx_return(step, freq):
+        sems = (tx_back_send, tx_back_recv)
+        return send_over("tx", step, freq, partial, landed, sems, ntx, nty)
+
+    def start_all(copy, size, freq):
+        for step in range(1, size):
+            copy(step, freq).start()
+
+    def await_all(copy, size, freq):
+        for step in range(1, size):
+            copy(step, freq).wait_recv()
+
+    greet(tx, ty, ntx, nty)
+    cols_out[...] = jnp.zeros_like(cols_out)
+    state, edges = heat_sweeps(
+        ntx, nty, heat, kind, nodes, factor, row_spots, col_spots, rows_out, rows_in, cols_out,
+        cols_in, edge_send, edge_recv,
+    )
+    warmed[...] = state
+    proportion[...] = jax.nn.sigmoid(
+        (of_kind(kind[...], threshold) - state) * (1.0 / ORDERING_SPREAD)
+    )
+
+    def layer_spectra(freqs):
+        def layer_part(part, carry):
+            values = [moment[part, sheet] * proportion[sheet] for sheet in range(sheets)]
+            for freq in freqs:
+                real = jnp.zeros((rows, width), jnp.float32)
+                imag = jnp.zeros((rows, width), jnp.float32)
+                for sheet in range(sheets):
+                    angle = 2.0 * math.pi * (sheet * freq % count) / count
+                    real = real + values[sheet] * math.cos(angle)
+                    imag = imag - values[sheet] * math.sin(angle)
+                layered[freq // own, freq % own, 0, part] = real
+                layered[freq // own, freq % own, 1, part] = imag
+                if 0 < freq < sheets:
+                    other = count - freq
+                    layered[other // own, other % own, 0, part] = real
+                    layered[other // own, other % own, 1, part] = -imag
+            return carry
+
+        lax.fori_loop(0, parts, layer_part, 0)
+
+    ready = set()
+    for freq in range(own):
+        needed = []
+        for line in range(sheets + 1):
+            if line not in ready and freq in (line % own, (count - line) % own):
+                needed.append(line)
+        if needed:
+            layer_spectra(needed)
+            ready.update(needed)
+        if freq < AHEAD:
+            start_all(tx_copy, ntx, freq)
+
+    def assemble(source, freq, size, high_ref, low_ref):
+        for index in range(size):
+            high, low = split(source[index, freq].reshape(2 * half, width))
+            high_ref[:, index * width : (index + 1) * width] = high
+            low_ref[:, index * width : (index + 1) * width] = low
+
+    def along(block):
+        result = product(along_high[...], along_low[...], to_high[block], to_low[block])
+        real = result[:half, :width] + result[half:, width:]
+        imag = result[half:, :width] - result[:half, width:]
+        return real.reshape(parts, rows, width), imag.reshape(parts, rows, width)
+
+    def forward_columns(freq):
+        await_all(tx_copy, ntx, freq)
+        if freq + AHEAD < own:
+            start_all(tx_copy, ntx, freq + AHEAD)
+        gathered[tx, freq] = layered[tx, freq]
+        assemble(gathered, freq, ntx, along_high, along_low)
+        if freq == 0:
+            loads[0].wait()
+            loads[1].wait()
+
+        def one(step, carry):
+            block = lax.rem(ty + step, nty)
+            real, imag = along(block)
+            blocks[block, freq, :, :, :width] = real
+            blocks[block, freq, :, :, width:] = imag
+            ty_copy(step, freq).start()
+            return carry
+
+        lax.fori_loop(1, nty, one, 0)
+        real, imag = along(ty)
+        arrived[ty, freq, :, :, :width] = real
+        arrived[ty, freq, :, :, width:] = imag
+
+    def through_rows(freq):
+        await_all(ty_copy, nty, freq)
+
+        def forward_rows(part, carry):
+            high, low = split(arrived[:, freq, part].reshape(total, 2 * width))
+            result = product(fwd_high[...], fwd_low[...], high, low)
+            top = 2 * total
+            spectra[part, :, :width] = result[:top, :width] + result[top:, width:]
+            spectra[part, :, width:] = result[:top, width:] - result[top:, :width]
+            return carry
+
+        lax.fori_loop(0, parts, forward_rows, 0)
+        if freq == 0:
+            loads[2].wait()
+        for part in range(parts):
+            sides = []
+            for side in range(2):
+                lanes = slice(side * width, (side + 1) * width)
+                sides.append(
+                    tensor[PAIRS[part][0], freq] * spectra[0, :, lanes]
+                    + tensor[PAIRS[part][1], freq] * spectra[1, :, lanes]
+                    + tensor[PAIRS[part][2], freq] * spectra[2, :, lanes]
+                )
+            high, low = split(jnp.concatenate(sides, axis=1))
+            result = product(back_high[...], back_low[...], high, low)
+            real = result[:total, :width] - result[total:, width:]
+            imag = result[:total, width:] + result[total:, :width]
+            field[:, freq, 0, part] = real.reshape(nty, rows, width)
+            field[:, freq, 1, part] = imag.reshape(nty, rows, width)
+        start_all(ty_return, nty, freq)
+        returned[ty, freq] = field[ty, freq]
+
+    def inverse(block):
+        result = product(inverse_high[...], inverse_low[...], from_high[block], from_low[block])
+        real = result[:half, :width] - result[half:, width:]
+        imag = result[:half, width:] + result[half:, :width]
+        return real.reshape(parts, rows, width), imag.reshape(parts, rows, width)
+
+    def inverse_columns(freq):
+        await_all(ty_return, nty, freq)
+        assemble(returned, freq, nty, inverse_high, inverse_low)
+        if freq == 0:
+            loads[3].wait()
+            loads[4].wait()
+
+        def one(step, carry):
+            block = lax.rem(tx + step, ntx)
+            partial[block, freq, 0], partial[block, freq, 1] = inverse(block)
+            tx_return(step, freq).start()
+            return carry
+
+        lax.fori_loop(1, ntx, one, 0)
+        landed[tx, freq, 0], landed[tx, freq, 1] = inverse(tx)
+
+    for turn in range(own + 3):
+        if turn < own:
+            forward_columns(turn)
+        if 0 <= turn - 1 < own:
+            through_rows(turn - 1)
+        if 0 <= turn - 3 < own:
+            inverse_columns(turn - 3)
+
+    scale = -1.0 / (count * 2 * total * 2 * ntx * width)
+    for freq in range(own):
+        await_all(tx_return, ntx, freq)
+
+        def back_layers(part, carry):
+            for sheet in range(sheets):
+                value = jnp.zeros((rows, width), jnp.float32) if freq == 0 else out[part, sheet]
+                for source in range(ntx):
+                    line = source * own + freq
+                    angle = 2.0 * math.pi * (sheet * line % count) / count
+                    value = value + landed[source, freq, 0, part] * (scale * math.cos(angle))
+                    value = value - landed[source, freq, 1, part] * (scale * math.sin(angle))
+                out[part, sheet] = value
+            return carry
+
+        lax.fori_loop(0, parts, back_layers, 0)
+
+    for edge in edges:
+        edge.wait_send()
+    for freq in range(own):
+        for copy, size in ((tx_copy, ntx), (ty_copy, nty), (ty_return, nty), (tx_return, ntx)):
+            for step in range(1, size):
+                copy(step, freq).wait_send()
+
+
+def everything(heat, kind, moment, stray_tensor, scalars, ntx, nty):
+    parts, sheets, rows, width = moment.shape
+    own = 2 * sheets // ntx
+    total, columns = nty * rows, ntx * width
+    forward = angles(2 * total, total, 2 * total)
+    forward = halves(np.concatenate([np.cos(forward), np.sin(forward)], axis=0))
+    back = angles(total, 2 * total, 2 * total)
+    back = halves(np.concatenate([np.cos(back), np.sin(back)], axis=0))
+    to_table = halves(blocked_pair(angles(columns, nty * width, 2 * columns), width))
+    from_table = halves(blocked_pair(angles(nty * width, columns, 2 * columns), width))
+    lines = 2 * parts * rows
+    dma = pltpu.SemaphoreType.DMA
+    anywhere = pl.BlockSpec(memory_space=pl.ANY)
+    over_tx = pltpu.VMEM((ntx, own, 2, parts, rows, width), jnp.float32)
+    over_ty = pltpu.VMEM((nty, own, parts, rows, 2 * width), jnp.float32)
+    back_ty = pltpu.VMEM((nty, own, 2, parts, rows, width), jnp.float32)
+    return pl.pallas_call(
+        functools.partial(whole_kernel, ntx, nty),
+        out_shape=(
+            jax.ShapeDtypeStruct(heat.shape, jnp.float32),
+            jax.ShapeDtypeStruct(moment.shape, jnp.float32),
+        ),
+        in_specs=[vmem()] * 3
+        + [pl.BlockSpec(memory_space=pltpu.SMEM)] * len(scalars)
+        + [vmem()] * 4
+        + [anywhere] * 5,
+        out_specs=(vmem(), vmem()),
+        scratch_shapes=[
+            pltpu.VMEM((sheets, rows, width), jnp.float32),
+            over_tx,
+            over_tx,
+            over_ty,
+            over_ty,
+            pltpu.VMEM((parts, 2 * total, 2 * width), jnp.float32),
+            back_ty,
+            back_ty,
+            over_tx,
+            over_tx,
+            pltpu.VMEM(stray_tensor.shape, jnp.float32),
+            pltpu.VMEM(to_table[0].shape, jnp.bfloat16),
+            pltpu.VMEM(to_table[1].shape, jnp.bfloat16),
+            pltpu.VMEM(from_table[0].shape, jnp.bfloat16),
+            pltpu.VMEM(from_table[1].shape, jnp.bfloat16),
+            pltpu.VMEM((lines, columns), jnp.bfloat16),
+            pltpu.VMEM((lines, columns), jnp.bfloat16),
+            pltpu.VMEM((lines, nty * width), jnp.bfloat16),
+            pltpu.VMEM((lines, nty * width), jnp.bfloat16),
+            *edge_scratch(sheets, rows, width),
+            dma((5,)),
+            dma((own, ntx)),
+            dma((own, ntx)),
+            dma((own, nty)),
+            dma((own, nty)),
+            dma((own, nty)),
+            dma((own, nty)),
+            dma((own, ntx)),
+            dma((own, ntx)),
+        ],
+        compiler_params=params(2),
+        name="demagnetize",
+    )(heat, kind, moment, *scalars, *forward, *back, stray_tensor, *to_table, *from_table)
+
+
 def local(
     reduced_heat,
     substance_kind,
@@ -501,6 +783,10 @@
         beam_transverse_spot,
         beam_downtrack_spot,
     )
+    if 16 * ntx * nty * reduced_heat.shape[2] ** 2 <= TABLE_BYTES:
+        return everything(
+            reduced_heat, substance_kind, moment_vector, stray_tensor, scalars, ntx, nty
+        )
     warmed_state, arrived = spectra_over_rows(
         reduced_heat, substance_kind, moment_vector, scalars, ntx, nty
     )

time: 137 us -> 120 us (0.88)
  Pallas kernels: 134 us -> 114 us
    pallas_call x2 -> x1, Pallas kernels: 134 us -> 114 us  [everything(): pl.pallas_call(functools.partial(whole_kernel, ntx, nty), out_shape=(jax....]
    unnamed x4 -> x2, local copies, waits for them, and re-layouts: 2.43 us -> 3.33 us
where the time goes in v3:
time: 120 us; the launch traced here: 118 us
  Pallas kernels  114 us (95%)
  local copies, waits for them, and re-layouts  3.33 us (3%)
    pallas_call x1, Pallas kernels, everything(): pl.pallas_call(functools.partial(whole_kernel, ntx, nty), out_shape=(jax....  114 us
    unnamed x2, local copies, waits for them, and re-layouts  3.33 us

profile of v3, /device:TPU:9, one launch (start us, length us, event | category | flops | bytes accessed | tf_op | source)
XLA Modules:
  0.0 118.4 jit_solution(10832395767470046962)
XLA Ops:
  0.6 114.5 %demagnetize.1 = (f32[8,32,128]{2,1,0:T(8,128)}, f32[3,8,32,128]{3,2,1,0:T(8,128)}) custom-call(f32[8,32,128]{2,1,0:T(8,128)} %heat.1, s32[8,32,128]{2,1,0:T(8,128)} %kind.1, f32[3,8,32,128]{3,2,1,0:T(8,128)} %moment.1, f32[16]{0:T(128)} %nodes.1, f32[4]{0:T(128)} %factor.1, f32[4]{0:T(128)} %threshold.1, s32[2]{0:T(128)} %row_spots.1, s32[2]{0:T(128)} %col_spots.1, ...), custom_call_target="tpu_custom_call" | custom-call | tf_op jit(solution)/shard_map/demagnetize/pallas_call | solution.py:720
  115.1 1.6 %copy.21 = f32[8,32,128]{2,1,0:T(8,128)} copy(f32[8,32,128]{2,1,0:T(8,128)} %get-tuple-element.4) | data formatting | bytes 262144
  116.7 1.8 %copy.22 = f32[3,8,32,128]{3,2,1,0:T(8,128)} copy(f32[3,8,32,128]{3,2,1,0:T(8,128)} %get-tuple-element.5) | data formatting | bytes 786432

commit v4 on v3

--- a/solution.py
+++ b/solution.py
@@ -484,57 +484,122 @@
     )(arrived, stray_tensor, *forward, *back, *x_table, layers.astype(np.float32))
 
 
+def deep_table(table, axis):
+    high, low = halves(table)
+    return np.concatenate([high, low, high], axis=axis)
+
+
+def deep_dot(table, high, low):
+    data = jnp.concatenate([high, high, low], axis=0)
+    return jnp.dot(table[...], data, preferred_element_type=jnp.float32)
+
+
+def row_units(own, rows, cut):
+    units = []
+    for freq in range(own):
+        pieces = 2 if freq == cut else 1
+        lines = rows // pieces
+        units += [(freq, piece * lines, lines) for piece in range(pieces)]
+    return units
+
+
+def send_rows(axis, step, unit, units, source, target, sems, ntx, nty):
+    tx, ty = lax.axis_index("tx"), lax.axis_index("ty")
+    freq, first, lines = units[unit]
+    if axis == "tx":
+        dest = lax.rem(tx + step, ntx)
+        mine, device = tx, (dest, ty)
+    else:
+        dest = lax.rem(ty + step, nty)
+        mine, device = ty, (tx, dest)
+    span = (slice(None),) * (len(source.shape) - 4) + (pl.ds(first, lines),)
+    return pltpu.make_async_remote_copy(
+        src_ref=source.at[(dest, freq) + span],
+        dst_ref=target.at[(mine, freq) + span],
+        send_sem=sems[0].at[unit, step],
+        recv_sem=sems[1].at[unit, step],
+        device_id=device,
+        device_id_type=MESH,
+    )
+
+
+def settle(*values):
+    def kernel(*refs):
+        count = len(values)
+        sems = refs[-1]
+        copies = [
+            pltpu.make_async_copy(refs[index], refs[count + index], sems.at[index])
+            for index in range(count)
+        ]
+        for copy in copies:
+            copy.start()
+        for copy in copies:
+            copy.wait()
+
+    anywhere = pl.BlockSpec(memory_space=pl.ANY)
+    return pl.pallas_call(
+        kernel,
+        out_shape=tuple(jax.ShapeDtypeStruct(value.shape, value.dtype) for value in values),
+        in_specs=[anywhere] * len(values),
+        out_specs=(anywhere,) * len(values),
+        scratch_shapes=[pltpu.SemaphoreType.DMA((len(values),))],
+        name="settle",
+    )(*values)
+
+
 def whole_kernel(
-    ntx, nty, heat, kind, moment, nodes, factor, threshold, row_spots, col_spots, fwd_high, fwd_low,
-    back_high, back_low, tensor_hbm, to_high_hbm, to_low_hbm, from_high_hbm, from_low_hbm,
-    warmed, out, proportion, layered, gathered, blocks, arrived, spectra, field, returned, partial,
-    landed, tensor, to_high, to_low, from_high, from_low, along_high, along_low, inverse_high,
-    inverse_low, rows_out, rows_in, cols_out, cols_in, edge_send, edge_recv, local_sem, tx_send,
-    tx_recv, ty_send, ty_recv, ty_back_send, ty_back_recv, tx_back_send, tx_back_recv,
+    ntx, nty, heat, kind, nodes, factor, threshold, row_spots, col_spots, moment_hbm, to_hbm,
+    forward_hbm, tensor_hbm, back_hbm, from_hbm, warmed, out, proportion, layered, gathered,
+    blocks, arrived, spectra, field, returned, partial, landed, moment, to_table, forward_table,
+    tensor, back_table, from_table, along_input, inverse_input, rows_out, rows_in, cols_out,
+    cols_in, edge_send, edge_recv, local_sem, tx_send, tx_recv, ty_send, ty_recv, ty_back_send,
+    ty_back_recv, tx_back_send, tx_back_recv,
 ):
     tx, ty = lax.axis_index("tx"), lax.axis_index("ty")
     parts, sheets, rows, width = moment.shape
     count = 2 * sheets
     own = count // ntx
     total = nty * rows
-    half = parts * rows
+    ahead, behind = row_units(own, rows, 0), row_units(own, rows, own - 1)
     loads = [
         pltpu.make_async_copy(source, target, local_sem.at[index])
         for index, (source, target) in enumerate(
             (
-                (to_high_hbm, to_high),
-                (to_low_hbm, to_low),
+                (moment_hbm, moment),
+                (to_hbm, to_table),
+                (forward_hbm, forward_table),
                 (tensor_hbm, tensor),
-                (from_high_hbm, from_high),
-                (from_low_hbm, from_low),
+                (back_hbm, back_table),
+                (from_hbm, from_table),
             )
         )
     ]
     for load in loads:
         load.start()
 
-    def tx_copy(step, freq):
+    def tx_copy(step, unit):
         sems = (tx_send, tx_recv)
-        return send_over("tx", step, freq, layered, gathered, sems, ntx, nty)
-
-    def ty_copy(step, freq):
-        return send_over("ty", step, freq, blocks, arrived, (ty_send, ty_recv), ntx, nty)
-
-    def ty_return(step, freq):
+        return send_rows("tx", step, unit, ahead, layered, gathered, sems, ntx, nty)
+
+    def ty_copy(step, unit):
+        sems = (ty_send, ty_recv)
+        return send_rows("ty", step, unit, ahead, blocks, arrived, sems, ntx, nty)
+
+    def ty_return(step, unit):
         sems = (ty_back_send, ty_back_recv)
-        return send_over("ty", step, freq, field, returned, sems, ntx, nty)
-
-    def tx_return(step, freq):
+        return send_rows("ty", step, unit, behind, field, returned, sems, ntx, nty)
+
+    def tx_return(step, unit):
         sems = (tx_back_send, tx_back_recv)
-        return send_over("tx", step, freq, partial, landed, sems, ntx, nty)
-
-    def start_all(copy, size, freq):
+        return send_rows("tx", step, unit, behind, partial, landed, sems, ntx, nty)
+
+    def start_all(copy, size, unit):
         for step in range(1, size):
-            copy(step, freq).start()
-
-    def await_all(copy, size, freq):
+            copy(step, unit).start()
+
+    def await_all(copy, size, unit):
         for step in range(1, size):
-            copy(step, freq).wait_recv()
+            copy(step, unit).wait_recv()
 
     greet(tx, ty, ntx, nty)
     cols_out[...] = jnp.zeros_like(cols_out)
@@ -567,6 +632,7 @@
 
         lax.fori_loop(0, parts, layer_part, 0)
 
+    loads[0].wait()
     ready = set()
     for freq in range(own):
         needed = []
@@ -576,58 +642,68 @@
         if needed:
             layer_spectra(needed)
             ready.update(needed)
-        if freq < AHEAD:
-            start_all(tx_copy, ntx, freq)
-
-    def assemble(source, freq, size, high_ref, low_ref):
+        for unit in range(AHEAD):
+            if ahead[unit][0] == freq:
+                start_all(tx_copy, ntx, unit)
+
+    def assemble(source, piece, size, target):
+        freq, first, lines = piece
+        depth = size * width
         for index in range(size):
-            high, low = split(source[index, freq].reshape(2 * half, width))
-            high_ref[:, index * width : (index + 1) * width] = high
-            low_ref[:, index * width : (index + 1) * width] = low
-
-    def along(block):
-        result = product(along_high[...], along_low[...], to_high[block], to_low[block])
-        real = result[:half, :width] + result[half:, width:]
-        imag = result[half:, :width] - result[:half, width:]
-        return real.reshape(parts, rows, width), imag.reshape(parts, rows, width)
-
-    def forward_columns(freq):
-        await_all(tx_copy, ntx, freq)
-        if freq + AHEAD < own:
-            start_all(tx_copy, ntx, freq + AHEAD)
-        gathered[tx, freq] = layered[tx, freq]
-        assemble(gathered, freq, ntx, along_high, along_low)
-        if freq == 0:
-            loads[0].wait()
+            value = source[index, freq, :, :, first : first + lines]
+            high, low = split(value.reshape(2 * parts * lines, width))
+            for place, half in enumerate((high, high, low)):
+                start = place * depth + index * width
+                target[: 2 * parts * lines, start : start + width] = half
+
+    def multiply(source, table, lines, sign):
+        half = parts * lines
+        result = jnp.dot(source[: 2 * half], table, preferred_element_type=jnp.float32)
+        real = result[:half, :width] + sign * result[half:, width:]
+        imag = result[half:, :width] - sign * result[:half, width:]
+        return real.reshape(parts, lines, width), imag.reshape(parts, lines, width)
+
+    def forward_columns(unit):
+        freq, first, lines = ahead[unit]
+        span = slice(first, first + lines)
+        await_all(tx_copy, ntx, unit)
+        if unit + AHEAD < len(ahead):
+            start_all(tx_copy, ntx, unit + AHEAD)
+        gathered[tx, freq, :, :, span] = layered[tx, freq, :, :, span]
+        assemble(gathered, ahead[unit], ntx, along_input)
+        if unit == 0:
             loads[1].wait()
 
         def one(step, carry):
             block = lax.rem(ty + step, nty)
-            real, imag = along(block)
-            blocks[block, freq, :, :, :width] = real
-            blocks[block, freq, :, :, width:] = imag
-            ty_copy(step, freq).start()
+            real, imag = multiply(along_input, to_table[block], lines, 1.0)
+            blocks[block, freq, :, span, :width] = real
+            blocks[block, freq, :, span, width:] = imag
+            ty_copy(step, unit).start()
             return carry
 
         lax.fori_loop(1, nty, one, 0)
-        real, imag = along(ty)
-        arrived[ty, freq, :, :, :width] = real
-        arrived[ty, freq, :, :, width:] = imag
+        real, imag = multiply(along_input, to_table[ty], lines, 1.0)
+        arrived[ty, freq, :, span, :width] = real
+        arrived[ty, freq, :, span, width:] = imag
 
     def through_rows(freq):
-        await_all(ty_copy, nty, freq)
+        for unit, piece in enumerate(ahead):
+            if piece[0] == freq:
+                await_all(ty_copy, nty, unit)
+        if freq == 0:
+            for load in loads[2:5]:
+                load.wait()
 
         def forward_rows(part, carry):
             high, low = split(arrived[:, freq, part].reshape(total, 2 * width))
-            result = product(fwd_high[...], fwd_low[...], high, low)
+            result = deep_dot(forward_table, high, low)
             top = 2 * total
             spectra[part, :, :width] = result[:top, :width] + result[top:, width:]
             spectra[part, :, width:] = result[:top, width:] - result[top:, :width]
             return carry
 
         lax.fori_loop(0, parts, forward_rows, 0)
-        if freq == 0:
-            loads[2].wait()
         for part in range(parts):
             sides = []
             for side in range(2):
@@ -638,67 +714,73 @@
                     + tensor[PAIRS[part][2], freq] * spectra[2, :, lanes]
                 )
             high, low = split(jnp.concatenate(sides, axis=1))
-            result = product(back_high[...], back_low[...], high, low)
+            result = deep_dot(back_table, high, low)
             real = result[:total, :width] - result[total:, width:]
             imag = result[:total, width:] + result[total:, :width]
             field[:, freq, 0, part] = real.reshape(nty, rows, width)
             field[:, freq, 1, part] = imag.reshape(nty, rows, width)
-        start_all(ty_return, nty, freq)
+        for unit, piece in enumerate(behind):
+            if piece[0] == freq:
+                start_all(ty_return, nty, unit)
         returned[ty, freq] = field[ty, freq]
 
-    def inverse(block):
-        result = product(inverse_high[...], inverse_low[...], from_high[block], from_low[block])
-        real = result[:half, :width] - result[half:, width:]
-        imag = result[:half, width:] + result[half:, :width]
-        return real.reshape(parts, rows, width), imag.reshape(parts, rows, width)
-
-    def inverse_columns(freq):
-        await_all(ty_return, nty, freq)
-        assemble(returned, freq, nty, inverse_high, inverse_low)
-        if freq == 0:
-            loads[3].wait()
-            loads[4].wait()
+    def inverse_columns(unit):
+        freq, first, lines = behind[unit]
+        span = slice(first, first + lines)
+        await_all(ty_return, nty, unit)
+        assemble(returned, behind[unit], nty, inverse_input)
+        if unit == 0:
+            loads[5].wait()
 
         def one(step, carry):
             block = lax.rem(tx + step, ntx)
-            partial[block, freq, 0], partial[block, freq, 1] = inverse(block)
-            tx_return(step, freq).start()
+            real, imag = multiply(inverse_input, from_table[block], lines, -1.0)
+            partial[block, freq, 0, :, span] = real
+            partial[block, freq, 1, :, span] = imag
+            tx_return(step, unit).start()
             return carry
 
         lax.fori_loop(1, ntx, one, 0)
-        landed[tx, freq, 0], landed[tx, freq, 1] = inverse(tx)
+        real, imag = multiply(inverse_input, from_table[tx], lines, -1.0)
+        landed[tx, freq, 0, :, span] = real
+        landed[tx, freq, 1, :, span] = imag
 
     for turn in range(own + 3):
-        if turn < own:
-            forward_columns(turn)
+        for unit, piece in enumerate(ahead):
+            if piece[0] == turn:
+                forward_columns(unit)
         if 0 <= turn - 1 < own:
             through_rows(turn - 1)
-        if 0 <= turn - 3 < own:
-            inverse_columns(turn - 3)
+        for unit, piece in enumerate(behind):
+            if piece[0] == turn - 3:
+                inverse_columns(unit)
 
     scale = -1.0 / (count * 2 * total * 2 * ntx * width)
-    for freq in range(own):
-        await_all(tx_return, ntx, freq)
+    for unit, (freq, first, lines) in enumerate(behind):
+        span = slice(first, first + lines)
+        await_all(tx_return, ntx, unit)
 
         def back_layers(part, carry):
             for sheet in range(sheets):
-                value = jnp.zeros((rows, width), jnp.float32) if freq == 0 else out[part, sheet]
+                value = jnp.zeros((lines, width), jnp.float32)
+                if freq > 0:
+                    value = out[part, sheet, span]
                 for source in range(ntx):
                     line = source * own + freq
                     angle = 2.0 * math.pi * (sheet * line % count) / count
-                    value = value + landed[source, freq, 0, part] * (scale * math.cos(angle))
-                    value = value - landed[source, freq, 1, part] * (scale * math.sin(angle))
-                out[part, sheet] = value
+                    value = value + landed[source, freq, 0, part, span] * (scale * math.cos(angle))
+                    value = value - landed[source, freq, 1, part, span] * (scale * math.sin(angle))
+                out[part, sheet, span] = value
             return carry
 
         lax.fori_loop(0, parts, back_layers, 0)
 
     for edge in edges:
         edge.wait_send()
-    for freq in range(own):
+    for unit in range(len(ahead)):
         for copy, size in ((tx_copy, ntx), (ty_copy, nty), (ty_return, nty), (tx_return, ntx)):
             for step in range(1, size):
-                copy(step, freq).wait_send()
+                copy(step, unit).wait_send()
 
 
 def everything(heat, kind, moment, stray_tensor, scalars, ntx, nty):
@@ -706,27 +788,27 @@
     own = 2 * sheets // ntx
     total, columns = nty * rows, ntx * width
     forward = angles(2 * total, total, 2 * total)
-    forward = halves(np.concatenate([np.cos(forward), np.sin(forward)], axis=0))
+    forward = deep_table(np.concatenate([np.cos(forward), np.sin(forward)], axis=0), 1)
     back = angles(total, 2 * total, 2 * total)
-    back = halves(np.concatenate([np.cos(back), np.sin(back)], axis=0))
-    to_table = halves(blocked_pair(angles(columns, nty * width, 2 * columns), width))
-    from_table = halves(blocked_pair(angles(nty * width, columns, 2 * columns), width))
+    back = deep_table(np.concatenate([np.cos(back), np.sin(back)], axis=0), 1)
+    to_table = deep_table(blocked_pair(angles(columns, nty * width, 2 * columns), width), 1)
+    from_table = deep_table(blocked_pair(angles(nty * width, columns, 2 * columns), width), 1)
     lines = 2 * parts * rows
     dma = pltpu.SemaphoreType.DMA
     anywhere = pl.BlockSpec(memory_space=pl.ANY)
     over_tx = pltpu.VMEM((ntx, own, 2, parts, rows, width), jnp.float32)
     over_ty = pltpu.VMEM((nty, own, parts, rows, 2 * width), jnp.float32)
     back_ty = pltpu.VMEM((nty, own, 2, parts, rows, width), jnp.float32)
-    return pl.pallas_call(
+    units = len(row_units(own, rows, 0))
+    return settle(*pl.pallas_call(
         functools.partial(whole_kernel, ntx, nty),
         out_shape=(
             jax.ShapeDtypeStruct(heat.shape, jnp.float32),
             jax.ShapeDtypeStruct(moment.shape, jnp.float32),
         ),
-        in_specs=[vmem()] * 3
+        in_specs=[vmem()] * 2
         + [pl.BlockSpec(memory_space=pltpu.SMEM)] * len(scalars)
-        + [vmem()] * 4
-        + [anywhere] * 5,
+        + [anywhere] * 6,
         out_specs=(vmem(), vmem()),
         scratch_shapes=[
             pltpu.VMEM((sheets, rows, width), jnp.float32),
@@ -739,29 +821,28 @@
             back_ty,
             over_tx,
             over_tx,
+            pltpu.VMEM(moment.shape, jnp.float32),
+            pltpu.VMEM(to_table.shape, jnp.bfloat16),
+            pltpu.VMEM(forward.shape, jnp.bfloat16),
             pltpu.VMEM(stray_tensor.shape, jnp.float32),
-            pltpu.VMEM(to_table[0].shape, jnp.bfloat16),
-            pltpu.VMEM(to_table[1].shape, jnp.bfloat16),
-            pltpu.VMEM(from_table[0].shape, jnp.bfloat16),
-            pltpu.VMEM(from_table[1].shape, jnp.bfloat16),
-            pltpu.VMEM((lines, columns), jnp.bfloat16),
-            pltpu.VMEM((lines, columns), jnp.bfloat16),
-            pltpu.VMEM((lines, nty * width), jnp.bfloat16),
-            pltpu.VMEM((lines, nty * width), jnp.bfloat16),
+            pltpu.VMEM(back.shape, jnp.bfloat16),
+            pltpu.VMEM(from_table.shape, jnp.bfloat16),
+            pltpu.VMEM((lines, 3 * columns), jnp.bfloat16),
+            pltpu.VMEM((lines, 3 * nty * width), jnp.bfloat16),
             *edge_scratch(sheets, rows, width),
-            dma((5,)),
-            dma((own, ntx)),
-            dma((own, ntx)),
-            dma((own, nty)),
-            dma((own, nty)),
-            dma((own, nty)),
-            dma((own, nty)),
-            dma((own, ntx)),
-            dma((own, ntx)),
+            dma((6,)),
+            dma((units, ntx)),
+            dma((units, ntx)),
+            dma((units, nty)),
+            dma((units, nty)),
+            dma((units, nty)),
+            dma((units, nty)),
+            dma((units, ntx)),
+            dma((units, ntx)),
         ],
         compiler_params=params(2),
         name="demagnetize",
-    )(heat, kind, moment, *scalars, *forward, *back, stray_tensor, *to_table, *from_table)
+    )(heat, kind, *scalars, moment, to_table, forward, stray_tensor, back, from_table))
 
 
 def local(

time: 120 us -> 133 us (1.11)
  Pallas kernels: 114 us -> 131 us
  local copies, waits for them, and re-layouts: 3.33 us -> 0 us
    pallas_call x0 -> x1, Pallas kernels: none -> 17 us  [settle(): pl.pallas_call(kernel, out_shape=tuple((jax.ShapeDtypeStruct(value.shape,...]
    unnamed x2 -> x0, local copies, waits for them, and re-layouts: 3.33 us -> none
where the time goes in v4:
time: 133 us; the launch traced here: 131 us
  Pallas kernels  131 us (98%)
    pallas_call x1, Pallas kernels, everything(): pl.pallas_call(functools.partial(whole_kernel, ntx, nty), out_shape=(jax....  114 us
    pallas_call x1, Pallas kernels, settle(): pl.pallas_call(kernel, out_shape=tuple((jax.ShapeDtypeStruct(value.shape,...  17 us

profile of v4, /device:TPU:9, one launch (start us, length us, event | category | flops | bytes accessed | tf_op | source)
XLA Modules:
  0.0 131.4 jit_solution(13170729301166260956)
XLA Ops:
  0.6 113.8 %demagnetize.1 = (f32[8,32,128]{2,1,0:T(8,128)}, f32[3,8,32,128]{3,2,1,0:T(8,128)}) custom-call(f32[8,32,128]{2,1,0:T(8,128)} %heat.1, s32[8,32,128]{2,1,0:T(8,128)} %kind.1, f32[16]{0:T(128)} %nodes.1, f32[4]{0:T(128)} %factor.1, f32[4]{0:T(128)} %threshold.1, s32[2]{0:T(128)} %row_spots.1, s32[2]{0:T(128)} %col_spots.1, f32[3,8,32,128]{3,2,1,0:T(8,128)} %moment_hbm.1, ...), custom_call_target="tpu_custom_call" | custom-call | tf_op jit(solution)/shard_map/demagnetize/pallas_call | solution.py:803
  114.4 17.0 %settle.1 = (f32[8,32,128]{2,1,0:T(8,128)}, f32[3,8,32,128]{3,2,1,0:T(8,128)}) custom-call(f32[8,32,128]{2,1,0:T(8,128)} %get-tuple-element.4.refs_0_, f32[3,8,32,128]{3,2,1,0:T(8,128)} %get-tuple-element.5.refs_1_), custom_call_target="tpu_custom_call" | custom-call | tf_op jit(solution)/shard_map/settle/pallas_call | solution.py:540

commit v5 on v4

--- a/solution.py
+++ b/solution.py
@@ -503,6 +503,26 @@
     return units
 
 
+def flip(index, mask, size):
+    result, bit = 0, 1
+    while bit < size:
+        result = result + (index // bit + mask // bit) % 2 * bit
+        bit *= 2
+    return result
+
+
+def swapped(mask):
+    return mask - mask % 8 + mask % 2 + mask // 2 % 2 * 4 + mask // 4 % 2 * 2
+
+
+def mask_at(step, core, size):
+    order = [2, 4, 3, 5, 6, 7, 1] if size == 8 else list(range(size - 1, 0, -1))
+    mask = order[0]
+    for place, value in enumerate(order):
+        mask = jnp.where(step == place + 1, value, mask)
+    return jnp.where(core == 0, mask, swapped(mask)) if size == 8 else mask
+
+
 def send_rows(axis, step, unit, units, source, target, sems, ntx, nty):
     tx, ty = lax.axis_index("tx"), lax.axis_index("ty")
     freq, first, lines = units[unit]
@@ -510,7 +530,7 @@
         dest = lax.rem(tx + step, ntx)
         mine, device = tx, (dest, ty)
     else:
-        dest = lax.rem(ty + step, nty)
+        dest = flip(ty, step, nty)
         mine, device = ty, (tx, dest)
     span = (slice(None),) * (len(source.shape) - 4) + (pl.ds(first, lines),)
     return pltpu.make_async_remote_copy(
@@ -525,24 +545,14 @@
 
 def settle(*values):
     def kernel(*refs):
-        count = len(values)
-        sems = refs[-1]
-        copies = [
-            pltpu.make_async_copy(refs[index], refs[count + index], sems.at[index])
-            for index in range(count)
-        ]
-        for copy in copies:
-            copy.start()
-        for copy in copies:
-            copy.wait()
-
-    anywhere = pl.BlockSpec(memory_space=pl.ANY)
+        for index in range(len(values)):
+            refs[len(values) + index][...] = refs[index][...]
+
     return pl.pallas_call(
         kernel,
         out_shape=tuple(jax.ShapeDtypeStruct(value.shape, value.dtype) for value in values),
-        in_specs=[anywhere] * len(values),
-        out_specs=(anywhere,) * len(values),
-        scratch_shapes=[pltpu.SemaphoreType.DMA((len(values),))],
+        in_specs=[vmem()] * len(values),
+        out_specs=(vmem(),) * len(values),
         name="settle",
     )(*values)
 
@@ -675,11 +685,12 @@
             loads[1].wait()
 
         def one(step, carry):
-            block = lax.rem(ty + step, nty)
+            mask = mask_at(step, ty % 2, nty)
+            block = flip(ty, mask, nty)
             real, imag = multiply(along_input, to_table[block], lines, 1.0)
             blocks[block, freq, :, span, :width] = real
             blocks[block, freq, :, span, width:] = imag
-            ty_copy(step, unit).start()
+            ty_copy(mask, unit).start()
             return carry
 
         lax.fori_loop(1, nty, one, 0)
@@ -721,7 +732,8 @@
             field[:, freq, 1, part] = imag.reshape(nty, rows, width)
         for unit, piece in enumerate(behind):
             if piece[0] == freq:
-                start_all(ty_return, nty, unit)
+                for step in range(1, nty):
+                    ty_return(mask_at(step, ty % 2, nty), unit).start()
         returned[ty, freq] = field[ty, freq]
 
     def inverse_columns(unit):

time: 133 us -> 120 us (0.902)
  Pallas kernels: 131 us -> 118 us
    pallas_call x1, Pallas kernels: 17 us -> 1.87 us  [settle(): pl.pallas_call(kernel, out_shape=tuple((jax.ShapeDtypeStruct(value.shape,...]
    pallas_call x1, Pallas kernels: 114 us -> 116 us  [everything(): pl.pallas_call(functools.partial(whole_kernel, ntx, nty), out_shape=(jax....]
where the time goes in v5:
time: 120 us; the launch traced here: 119 us
  Pallas kernels  118 us (98%)
    pallas_call x1, Pallas kernels, everything(): pl.pallas_call(functools.partial(whole_kernel, ntx, nty), out_shape=(jax....  116 us

profile of v5, /device:TPU:9, one launch (start us, length us, event | category | flops | bytes accessed | tf_op | source)
XLA Modules:
  0.0 118.7 jit_solution(2170540602576259516)
XLA Ops:
  0.6 116.2 %demagnetize.1 = (f32[8,32,128]{2,1,0:T(8,128)}, f32[3,8,32,128]{3,2,1,0:T(8,128)}) custom-call(f32[8,32,128]{2,1,0:T(8,128)} %heat.1, s32[8,32,128]{2,1,0:T(8,128)} %kind.1, f32[16]{0:T(128)} %nodes.1, f32[4]{0:T(128)} %factor.1, f32[4]{0:T(128)} %threshold.1, s32[2]{0:T(128)} %row_spots.1, s32[2]{0:T(128)} %col_spots.1, f32[3,8,32,128]{3,2,1,0:T(8,128)} %moment_hbm.1, ...), custom_call_target="tpu_custom_call" | custom-call | tf_op jit(solution)/shard_map/demagnetize/pallas_call | solution.py:815
  116.8 1.9 %settle.1 = (f32[8,32,128]{2,1,0:T(8,128)}, f32[3,8,32,128]{3,2,1,0:T(8,128)}) custom-call(f32[8,32,128]{2,1,0:T(8,128)} %get-tuple-element.4.refs_0_, f32[3,8,32,128]{3,2,1,0:T(8,128)} %get-tuple-element.5.refs_1_), custom_call_target="tpu_custom_call" | custom-call | tf_op jit(solution)/shard_map/settle/pallas_call | solution.py:551

commit v6 on v3

--- a/solution.py
+++ b/solution.py
@@ -23,7 +23,7 @@
 
 
 MESH = pl.DeviceIdType.MESH
-AHEAD = 2
+AHEAD = 4
 TABLE_BYTES = 16 * 1024 * 1024
 PAIRS = ((0, 3, 4), (3, 1, 5), (4, 5, 2))
 
@@ -576,7 +576,7 @@
         if needed:
             layer_spectra(needed)
             ready.update(needed)
-        if freq < AHEAD:
+        if freq < min(AHEAD, own):
             start_all(tx_copy, ntx, freq)
 
     def assemble(source, freq, size, high_ref, low_ref):
@@ -701,6 +701,20 @@
                 copy(step, freq).wait_send()
 
 
+def settle(*values):
+    def kernel(*refs):
+        for index in range(len(values)):
+            refs[len(values) + index][...] = refs[index][...]
+
+    return pl.pallas_call(
+        kernel,
+        out_shape=tuple(jax.ShapeDtypeStruct(value.shape, value.dtype) for value in values),
+        in_specs=[vmem()] * len(values),
+        out_specs=(vmem(),) * len(values),
+        name="settle",
+    )(*values)
+
+
 def everything(heat, kind, moment, stray_tensor, scalars, ntx, nty):
     parts, sheets, rows, width = moment.shape
     own = 2 * sheets // ntx
@@ -717,7 +731,7 @@
     over_tx = pltpu.VMEM((ntx, own, 2, parts, rows, width), jnp.float32)
     over_ty = pltpu.VMEM((nty, own, parts, rows, 2 * width), jnp.float32)
     back_ty = pltpu.VMEM((nty, own, 2, parts, rows, width), jnp.float32)
-    return pl.pallas_call(
+    return settle(*pl.pallas_call(
         functools.partial(whole_kernel, ntx, nty),
         out_shape=(
             jax.ShapeDtypeStruct(heat.shape, jnp.float32),
@@ -761,7 +775,7 @@
         ],
         compiler_params=params(2),
         name="demagnetize",
-    )(heat, kind, moment, *scalars, *forward, *back, stray_tensor, *to_table, *from_table)
+    )(heat, kind, moment, *scalars, *forward, *back, stray_tensor, *to_table, *from_table))
 
 
 def local(

time: 120 us -> 118 us (0.983)
  local copies, waits for them, and re-layouts: 3.33 us -> 0 us
  Pallas kernels: 114 us -> 116 us
    unnamed x2 -> x0, local copies, waits for them, and re-layouts: 3.33 us -> none
    pallas_call x0 -> x1, Pallas kernels: none -> 1.87 us  [settle(): pl.pallas_call(kernel, out_shape=tuple((jax.ShapeDtypeStruct(value.shape,...]
where the time goes in v6:
time: 118 us; the launch traced here: 117 us
  Pallas kernels  116 us (98%)
    pallas_call x1, Pallas kernels, everything(): pl.pallas_call(functools.partial(whole_kernel, ntx, nty), out_shape=(jax....  115 us

profile of v6, /device:TPU:9, one launch (start us, length us, event | category | flops | bytes accessed | tf_op | source)
XLA Modules:
  0.0 117.1 jit_solution(5774689229145040630)
XLA Ops:
  0.6 114.6 %demagnetize.1 = (f32[8,32,128]{2,1,0:T(8,128)}, f32[3,8,32,128]{3,2,1,0:T(8,128)}) custom-call(f32[8,32,128]{2,1,0:T(8,128)} %heat.1, s32[8,32,128]{2,1,0:T(8,128)} %kind.1, f32[3,8,32,128]{3,2,1,0:T(8,128)} %moment.1, f32[16]{0:T(128)} %nodes.1, f32[4]{0:T(128)} %factor.1, f32[4]{0:T(128)} %threshold.1, s32[2]{0:T(128)} %row_spots.1, s32[2]{0:T(128)} %col_spots.1, ...), custom_call_target="tpu_custom_call" | custom-call | tf_op jit(solution)/shard_map/demagnetize/pallas_call | solution.py:734
  115.2 1.9 %settle.1 = (f32[8,32,128]{2,1,0:T(8,128)}, f32[3,8,32,128]{3,2,1,0:T(8,128)}) custom-call(f32[8,32,128]{2,1,0:T(8,128)} %get-tuple-element.4.refs_0_, f32[3,8,32,128]{3,2,1,0:T(8,128)} %get-tuple-element.5.refs_1_), custom_call_target="tpu_custom_call" | custom-call | tf_op jit(solution)/shard_map/settle/pallas_call | solution.py:709
